TPU v7x, 512 devices: a whole 4x8x8 slice. The times are simulated.
512 devices in a mesh: rep: 8 (over x, core), seq: 64 (over z, y).
Axes of the slice: x: 4, y: 8, z: 8, core: 2. Of those that a mesh axis runs over, the one named last changes fastest.
Arguments:
- latents: bfloat16 [32, 64, 64, 1152], P('rep', 'seq'), may hold values from -6 to 6
- destination: int32 [32], P('rep'), may hold values from 0 to 7, as said below
- token_counts: int32 [32, 64], P('rep', 'seq'), may hold values from 16 to 64, as said below
- frame_counts: int32 [32, 4], P('rep'), may hold values from 1 to 32, 64 in all within a row
- gains_spatial: float32 [3, 1152], replicated
- gains_temporal: float32 [3, 1152], replicated
- qkv_spatial: bfloat16 [1152, 1728], P(None, 'seq'), may hold values from -0.1875 to 0.1875
- proj_spatial: bfloat16 [576, 1152], P(None, 'seq'), may hold values from -0.25 to 0.25
- qkv_temporal: bfloat16 [1152, 1728], P(None, 'seq'), may hold values from -0.1875 to 0.1875
- proj_temporal: bfloat16 [576, 1152], P(None, 'seq'), may hold values from -0.25 to 0.25
- cotangent: bfloat16 [32, 64, 64, 1152], P('rep', 'seq'), may hold values from -6 to 6
Outputs:
- block_out: bfloat16 [32, 64, 64, 1152], P('rep', 'seq')
- latent_grad: bfloat16 [32, 64, 64, 1152], P('rep', 'seq')
- gain_grads: float32 [2, 3, 1152], replicated
Inputs may be any that keep to these rules, and one draw needn't show every extreme that they name: `destination`: every replica group receives exactly 4 bins; no replica group sends more than 1 of its bins to one replica group, and some replica group sends exactly 1 to one. `token_counts`: frame 0 of every bin has all 64 tokens valid.
All inputs are finite; a program needn't handle non-finite values.
Results may differ from a plain program's by a relative error of at most 0.035.
Values may be sent and summed in bfloat16 or wider, within the bound.
No kernel may reach another device: no remote copies, remote signals or barrier semaphores. Data moves between devices by JAX's collectives and lax.ppermute only.
A program may use at most 128 MiB of HBM per device.

v0:
```python
import math

import jax
import jax.numpy as jnp
from jax import lax
from jax.experimental import pallas as pl
from jax.experimental.pallas import tpu as pltpu
from jax.sharding import Mesh
from jax.sharding import PartitionSpec as P

HEADS = 8
HD = 72
INNER = HEADS * HD
SEQ = ("z", "y")
W_PAD = 1792
U_CUT = 640


def scores_of(q_ref, k_ref, head, allowed):
    rows = slice(HD * head, HD * head + HD)
    query = q_ref[rows, :].astype(jnp.bfloat16)
    keys = k_ref[rows, :].astype(jnp.bfloat16)
    raw = lax.dot_general(
        keys, query, (((0,), (0,)), ((), ())), preferred_element_type=jnp.float32
    )
    raw = jnp.where(allowed, raw * (1.0 / math.sqrt(HD)), -1000000000.0)
    expo = jnp.exp(raw - jnp.max(raw, axis=0, keepdims=True))
    weights = expo * (1.0 / jnp.sum(expo, axis=0, keepdims=True))
    return query, keys, weights


def normed_of(v_ref):
    wide = v_ref[...].astype(jnp.float32)
    scale = lax.rsqrt(jnp.mean(wide * wide, axis=1, keepdims=True) + 1e-06)
    return wide * scale, scale


def load_u(full_ref, u_ref):
    for part in range(8):
        block = full_ref[144 * part : 144 * part + 144, W_PAD : W_PAD + U_CUT].astype(jnp.float32)
        u_ref[72 * part : 72 * part + 72, :U_CUT] = block[:72]
        u_ref[72 * part : 72 * part + 72, U_CUT:] = block[72:, : 1152 - U_CUT]


def forward(v_ref, gains_ref, full_ref, key_label, query_label, out_ref, q_ref, k_ref, x_ref, o_ref, u_ref):
    normed, scale = normed_of(v_ref)

    def project(which, first, past):
        scaled = (normed * gains_ref[which : which + 1, :]).astype(jnp.bfloat16)
        made = jnp.dot(scaled, full_ref[:, first:past], preferred_element_type=jnp.float32)
        return jnp.transpose(made)

    q_ref[...] = project(0, 0, 640)[:INNER]
    k_ref[...] = project(1, 512, 1152)[64:]
    x_ref[...] = project(2, 1152, 1792)[:INNER]
    allowed = key_label == query_label
    for head in range(HEADS):
        rows = slice(HD * head, HD * head + HD)
        _, _, weights = scores_of(q_ref, k_ref, head, allowed)
        vals = x_ref[rows, :].astype(jnp.bfloat16)
        o_ref[rows, :] = jnp.dot(
            vals, weights.astype(jnp.bfloat16), preferred_element_type=jnp.float32
        )
    mixed = jnp.transpose(o_ref[...]).astype(jnp.bfloat16)
    made = jnp.dot(mixed, u_ref[...].astype(jnp.bfloat16), preferred_element_type=jnp.float32)
    out_ref[...] = (v_ref[...].astype(jnp.float32) + made).astype(jnp.bfloat16)


def backward(
    g_ref, v_ref, gains_ref, full_ref, key_label, query_label, grad_ref, gain_ref,
    q_ref, k_ref, x_ref, o_ref, u_ref, dq_ref, dk_ref, dx_ref,
):
    grad = g_ref[...]
    o_ref[...] = lax.dot_general(
        u_ref[...].astype(jnp.bfloat16),
        grad,
        (((1,), (1,)), ((), ())),
        preferred_element_type=jnp.float32,
    )
    zeros = jnp.zeros((640 - INNER, dq_ref.shape[1]), jnp.float32)
    dq_ref[INNER:, :] = zeros
    dk_ref[: 640 - INNER, :] = zeros
    dx_ref[INNER:, :] = zeros
    allowed = key_label == query_label
    over_lanes = (((1,), (1,)), ((), ()))
    for head in range(HEADS):
        low = HD * head
        rows = slice(low, low + HD)
        query, keys, weights = scores_of(q_ref, k_ref, head, allowed)
        vals = x_ref[rows, :].astype(jnp.bfloat16)
        d_out = o_ref[rows, :].astype(jnp.bfloat16)
        d_weights = lax.dot_general(
            vals, d_out, (((0,), (0,)), ((), ())), preferred_element_type=jnp.float32
        )
        along = jnp.sum(d_weights * weights, axis=0, keepdims=True)
        d_scores = weights * (d_weights - along) * (1.0 / math.sqrt(HD))
        d_scores = d_scores.astype(jnp.bfloat16)
        dq_ref[rows, :] = jnp.dot(keys, d_scores, preferred_element_type=jnp.float32)
        dk_ref[64 + low : 64 + low + HD, :] = lax.dot_general(
            query, d_scores, over_lanes, preferred_element_type=jnp.float32
        )
        dx_ref[rows, :] = lax.dot_general(
            d_out, weights.astype(jnp.bfloat16), over_lanes, preferred_element_type=jnp.float32
        )
    normed, scale = normed_of(v_ref)
    d_normed = None
    for which, (ref, first) in enumerate(((dq_ref, 0), (dk_ref, 512), (dx_ref, 1152))):
        made = jnp.transpose(ref[...]).astype(jnp.bfloat16)
        back = lax.dot_general(
            made, full_ref[:, first : first + 640], over_lanes, preferred_element_type=jnp.float32
        )
        gain_ref[which : which + 1, :] = jnp.sum(back * normed, axis=0, keepdims=True)
        term = back * gains_ref[which : which + 1, :]
        d_normed = term if d_normed is None else d_normed + term
    inward = jnp.mean(d_normed * normed, axis=1, keepdims=True)
    result = grad.astype(jnp.float32) + scale * (d_normed - normed * inward)
    grad_ref[...] = result.astype(jnp.bfloat16)


def spatial_forward_kernel(v, gains, full, lab_k, lab_q, mid, qkv, q, k, x, o, u):
    load_u(full, u)
    forward(v, gains, full, lab_k[...], lab_q[...], mid, q, k, x, o, u)
    for which, ref in enumerate((q, k, x)):
        qkv[which] = ref[...].astype(jnp.bfloat16)


def spatial_backward_kernel(
    g, v, gains, full, lab_k, lab_q, qkv, grad, gain, q, k, x, o, u, dq, dk, dx
):
    load_u(full, u)
    for which, ref in enumerate((q, k, x)):
        ref[...] = qkv[which].astype(jnp.float32)
    backward(g, v, gains, full, lab_k[...], lab_q[...], grad, gain, q, k, x, o, u, dq, dk, dx)


def temporal_kernel(
    g, v, gains, full, lab_k, lab_q, out, grad, gain, q, k, x, o, u, dq, dk, dx
):
    load_u(full, u)
    forward(v, gains, full, lab_k[...], lab_q[...], out, q, k, x, o, u)
    backward(g, v, gains, full, lab_k[...], lab_q[...], grad, gain, q, k, x, o, u, dq, dk, dx)


def call_kernel(kernel, outs, backs, name):
    rows = 256
    wide = pltpu.VMEM((INNER, rows), jnp.float32)
    scratch = [wide] * 4 + [pltpu.VMEM((INNER, 1152), jnp.float32)]
    if backs:
        scratch += [pltpu.VMEM((640, rows), jnp.float32)] * 3
    return pl.pallas_call(
        kernel,
        out_shape=outs,
        scratch_shapes=scratch,
        compiler_params=pltpu.CompilerParams(vmem_limit_bytes=50 * 1024 * 1024),
        cost_estimate=pl.CostEstimate(
            flops=int(6e9), bytes_accessed=int(8e6), transcendentals=int(5e5)
        ),
        name=name,
    )


ROWS_OUT = jax.ShapeDtypeStruct((256, 1152), jnp.bfloat16)
GAIN_OUT = jax.ShapeDtypeStruct((3, 1152), jnp.float32)
QKV_OUT = jax.ShapeDtypeStruct((3, 576, 256), jnp.bfloat16)


def exchange(rows, axes):
    return lax.all_to_all(rows, axes, split_axis=0, concat_axis=0, tiled=True)


def spread(value, axes):
    peers = lax.axis_size(axes)
    return exchange(jnp.broadcast_to(value[None], (peers,) + value.shape), axes)


def own_piece(qkv, proj, rep, groups):
    rows_w, rows_u = qkv.shape[0] // groups, proj.shape[0] // groups
    piece_w = lax.dynamic_slice(qkv.T, (0, rep * rows_w), (qkv.shape[1], rows_w)).reshape(-1)
    piece_u = lax.dynamic_slice(proj.T, (0, rep * rows_u), (proj.shape[1], rows_u)).reshape(-1)
    return jnp.concatenate([piece_w, piece_u])


def gather_weights(got, shard, shard_u, rows_w, rows_u):
    peers = got.shape[0]
    cut = shard * rows_w
    part_w = got[:, :cut].reshape(peers * shard, rows_w).T
    part_u = got[:, cut : cut + shard_u * rows_u].reshape(peers * shard_u, rows_u).T
    part_w = jnp.pad(part_w, ((0, 0), (0, W_PAD - part_w.shape[1])))
    low, high = part_u[:, :U_CUT], part_u[:, U_CUT:]
    high = jnp.pad(high, ((0, 0), (0, U_CUT - high.shape[1])))
    part = jnp.concatenate([part_w, jnp.concatenate([low, high], axis=0)], axis=1)
    full = lax.all_gather(part, "rep", axis=0, tiled=False)
    return full.reshape(full.shape[0] * full.shape[1], full.shape[2])


def local(
    latents,
    destination,
    token_counts,
    frame_counts,
    gains_spatial,
    gains_temporal,
    qkv_spatial,
    proj_spatial,
    qkv_temporal,
    proj_temporal,
    cotangent,
):
    bins_here, _, slots, width = latents.shape
    groups = lax.axis_size("rep")
    frames = lax.axis_size(SEQ)
    group = lax.axis_index("rep")
    place = lax.axis_index(SEQ)
    inner = proj_spatial.shape[0]
    tokens = bins_here * slots // frames
    rows = bins_here * slots
    sizes = (qkv_spatial.shape[1], proj_spatial.shape[1], width // groups, inner // groups)

    mine = jnp.concatenate([destination, token_counts[:, 0], frame_counts.reshape(-1)])
    mine = jnp.pad(mine.astype(jnp.bfloat16)[None], ((0, 15), (0, width - mine.shape[0])))
    sent = jnp.concatenate([cotangent.reshape(rows, width), mine], axis=0)
    shared = lax.all_gather(sent, "rep", axis=0, tiled=False)

    flat_s = own_piece(qkv_spatial, proj_spatial, group, groups)
    flat_s = jnp.pad(flat_s, (0, -flat_s.shape[0] % 256))
    got_s = spread(flat_s.reshape(2, -1), SEQ).reshape(frames, -1)
    full_s = gather_weights(got_s, *sizes)

    facts = shared[:, rows, :128].astype(jnp.int32)
    dest_all = facts[:, :bins_here]
    tokens_all = facts[:, bins_here : 2 * bins_here].reshape(-1)
    videos_all = facts[:, 2 * bins_here : 2 * bins_here + frame_counts.size]
    videos_all = videos_all.reshape(groups * bins_here, -1)
    group_ids = jnp.arange(groups, dtype=jnp.int32)
    bin_ids = jnp.arange(bins_here, dtype=jnp.int32)
    earlier = (dest_all[None] == destination[:, None, None]) & (
        group_ids[None, :, None] < group
    )
    rank = jnp.sum(earlier.astype(jnp.int32), axis=(1, 2))
    new_place = destination * bins_here + rank
    pick_new = (new_place[:, None] == jnp.arange(groups * bins_here, dtype=jnp.int32)).astype(
        jnp.int32
    )
    my_tokens = jnp.sum(pick_new * tokens_all[None], axis=1)
    my_videos = jnp.sum(pick_new[:, :, None] * videos_all[None], axis=1)
    comes = jnp.any(dest_all == group, axis=1).astype(jnp.int32)
    order = jnp.cumsum(comes) - 1
    source = ((order[None] == bin_ids[:, None]) & (comes[None] > 0)).astype(jnp.int32)
    from_group = jnp.sum(source * group_ids[None], axis=1)
    bin_there = jnp.sum((dest_all == group).astype(jnp.int32) * bin_ids[None], axis=1)
    from_bin = jnp.sum(source * bin_there[None], axis=1)

    cot_here = jnp.stack(
        [
            lax.dynamic_slice(shared, (destination[i], rank[i] * slots, 0), (1, slots, width))[0]
            for i in range(bins_here)
        ]
    )
    flat_t = own_piece(qkv_temporal, proj_temporal, group, groups).reshape(tokens, -1)
    flat_t = jnp.pad(flat_t, ((0, 0), (0, -flat_t.shape[1] % 128)))
    mixed = jnp.concatenate(
        [
            cot_here.reshape(frames, tokens, width),
            jnp.broadcast_to(flat_t[None], (frames,) + flat_t.shape),
        ],
        axis=2,
    )
    mixed = exchange(mixed, SEQ)
    cot_tokens = mixed[:, :, :width].reshape(rows, width)
    piece = sizes[0] * sizes[2] + sizes[1] * sizes[3]
    full_t = gather_weights(
        mixed[:, :, width : width + piece // tokens].reshape(frames, -1), *sizes
    )

    key_ok = jnp.arange(slots, dtype=jnp.int32)[None, :] < my_tokens[:, None]
    lab_k = jnp.where(key_ok, bin_ids[:, None], -1).reshape(rows, 1)
    lab_q = jnp.broadcast_to(bin_ids[:, None], (bins_here, slots)).reshape(1, rows)
    values = latents.reshape(rows, width)
    mid, qkv = call_kernel(spatial_forward_kernel, (ROWS_OUT, QKV_OUT), False, "spatial_forward")(
        values, gains_spatial, full_s, lab_k, lab_q
    )
    mid_tokens = exchange(mid.reshape(frames, tokens, width), SEQ).reshape(rows, width)

    ends = jnp.cumsum(my_videos, axis=1)
    video_id = jnp.sum(
        (ends[:, None, :] <= jnp.arange(frames, dtype=jnp.int32)[None, :, None]).astype(jnp.int32),
        axis=2,
    )
    row_bin = place * tokens // slots
    video_row = jnp.sum((bin_ids == row_bin).astype(jnp.int32)[:, None] * video_id, axis=0)
    lab_t = video_row[:, None] * tokens + jnp.arange(tokens, dtype=jnp.int32)[None]
    out_tokens, mid_grad_tokens, grad_temporal = call_kernel(
        temporal_kernel, (ROWS_OUT, ROWS_OUT, GAIN_OUT), True, "temporal"
    )(cot_tokens, mid_tokens, gains_temporal, full_t, lab_t.reshape(rows, 1), lab_t.reshape(1, rows))

    both = jnp.concatenate(
        [
            mid_grad_tokens.reshape(frames, tokens, width),
            out_tokens.reshape(frames, tokens, width),
        ],
        axis=1,
    )
    both = exchange(both, SEQ)
    mid_grad = both[:, :tokens].reshape(rows, width)
    outs = lax.all_gather(both[:, tokens:].reshape(rows, width), "rep", axis=0, tiled=False)
    block_out = jnp.stack(
        [
            lax.dynamic_slice(outs, (from_group[j], from_bin[j] * slots, 0), (1, slots, width))
            for j in range(bins_here)
        ]
    )
    latent_grad, grad_spatial = call_kernel(
        spatial_backward_kernel, (ROWS_OUT, GAIN_OUT), True, "spatial_backward"
    )(mid_grad, values, gains_spatial, full_s, lab_k, lab_q, qkv)
    sums = jnp.stack([grad_spatial, grad_temporal]).reshape(8, -1)
    for axis in ("y", "z", "rep"):
        sums = jnp.sum(spread(sums, axis), axis=0)
    gain_grads = sums.reshape((2,) + gains_spatial.shape)
    return (block_out, latent_grad.reshape(latents.shape), gain_grads)


def solution(mesh):
    rep, seq = mesh.devices.shape
    deep = Mesh(mesh.devices.reshape(rep, 8, seq // 8), ("rep", "z", "y"))
    in_specs = (
        P("rep", SEQ, None, None),
        P("rep"),
        P("rep", SEQ),
        P("rep", None),
        P(),
        P(),
        P(None, SEQ),
        P(None, SEQ),
        P(None, SEQ),
        P(None, SEQ),
        P("rep", SEQ, None, None),
    )
    out_specs = (P("rep", SEQ, None, None), P("rep", SEQ, None, None), P())
    return jax.shard_map(local, mesh=deep, in_specs=in_specs, out_specs=out_specs, check_vma=False)
```

profile of v0, /device:TPU:1, one launch (start us, length us, event | category | flops | bytes accessed | tf_op | source)
XLA Modules:
  0.0 281.2 jit_solution(13849972918063013747)
XLA Ops:
  9.4 2.0 pad_maximum_fusion.2
  11.4 0.8 dynamic-slice_bitcast_fusion.6
  12.3 0.8 dynamic-slice_bitcast_fusion.4
  13.7 36.8 %all_to_all.35 = bf16[64,2,2688]{2,1,0:T(2,128)(2,1)S(1)} all-to-all(bf16[64,2,2688]{2,1,0:T(2,128)(2,1)S(1)} %broadcast_in_dim.32), channel_id=1, replica_groups=mesh['rep'=8,'z'=8,'y'=8] {'z','y'}, dimensions={0} | all-to-all | bytes 1376256 | tf_op jit(solution)/shard_map/all_to_all | solution.py:168
  51.5 1.1 reshape.328
  52.8 0.9 fusion.8
  62.4 0.7 slice_convert_fusion
  66.6 1.2 constant_dynamic-slice_fusion.3
  68.8 42.0 %all_to_all.36 = bf16[64,4,2560]{2,1,0:T(4,128)(2,1)S(1)} all-to-all(bf16[64,4,2560]{2,1,0:T(4,128)(2,1)S(1)} %pad_maximum_fusion), channel_id=1, replica_groups=mesh['rep'=8,'z'=8,'y'=8] {'z','y'}, dimensions={0} | all-to-all | bytes 2621440 | tf_op jit(solution)/shard_map/all_to_all | solution.py:168
  112.4 1.1 reshape.335
  113.7 0.9 fusion.10
  115.3 7.5 %spatial_forward.1 = (bf16[256,1152]{1,0:T(8,128)(2,1)S(1)}, bf16[3,576,256]{2,1,0:T(8,128)(2,1)S(1)}) custom-call(bf16[256,1152]{1,0:T(8,128)(2,1)S(1)} %bitcast.57, f32[3,1152]{1,0:T(4,128)S(1)} %copy-done.2, bf16[1152,2432]{1,0:T(8,128)(2,1)} %all-gather.12.cloned.1.call-done.full, s32[256,1]{1,0:T(8,128)S(1)} %select_n.96.lab_k, s32[1,256]{1,0:T(1,128)S(1)} %reshape.331.lab_q), custom_call_target="tpu_custom_call" | custom-call | flops 6000000000 | bytes 8000000 | tf_op jit(solution)/shard_map/spatial_forward/pallas_call | solution.py:279
  122.8 1.1 reshape.332
  123.9 8.9 %all-to-all-start.2 = ((bf16[64,4,1152]{2,1,0:T(4,128)(2,1)}), bf16[64,4,1152]{2,1,0:T(4,128)(2,1)}, u32[]{:S(2)}, u32[]{:S(2)}) async-start(bf16[64,4,1152]{2,1,0:T(4,128)(2,1)} %reshape.332), calls=%async_computation.2 | async-start | bytes 1179648 | tf_op jit(solution)/shard_map/all_to_all | solution.py:168
  134.2 1.0 slice.129
  135.2 1.5 reshape.323.g
  136.7 12.6 %all-to-all-done.2 = bf16[64,4,1152]{2,1,0:T(4,128)(2,1)} async-done(((bf16[64,4,1152]{2,1,0:T(4,128)(2,1)}), bf16[64,4,1152]{2,1,0:T(4,128)(2,1)}, u32[]{:S(2)}, u32[]{:S(2)}) %all-to-all-start.2) | async-done | bytes 589856 | tf_op jit(solution)/shard_map/all_to_all | solution.py:168
  149.3 1.5 reshape.333.v
  150.7 3.6 %all-gather.14.cloned.1.call-done.full = bf16[1152,2432]{1,0:T(8,128)(2,1)} async-done(((bf16[144,2432]{1,0:T(8,128)(2,1)}), bf16[1152,2432]{1,0:T(8,128)(2,1)}) %all-gather.14.cloned.1.call-update) | async-done | bytes 5603344 | tf_op jit(solution)/shard_map/all_gather | solution.py:192
  154.3 13.6 %temporal.1 = (bf16[256,1152]{1,0:T(8,128)(2,1)S(1)}, bf16[256,1152]{1,0:T(8,128)(2,1)S(1)}, f32[3,1152]{1,0:T(4,128)S(1)}) custom-call(bf16[256,1152]{1,0:T(8,128)(2,1)S(1)} %reshape.323.g, bf16[256,1152]{1,0:T(8,128)(2,1)S(1)} %reshape.333.v, f32[3,1152]{1,0:T(4,128)S(1)} %copy-done.1, bf16[1152,2432]{1,0:T(8,128)(2,1)} %all-gather.14.cloned.1.call-done.full, ...), custom_call_target="tpu_custom_call" | custom-call | flops 6000000000 | bytes 8000000 | tf_op jit(solution)/shard_map/temporal/pallas_call | solution.py:292
  168.8 43.7 %all_to_all.37 = bf16[64,8,1152]{2,1,0:T(8,128)(2,1)S(1)} all-to-all(bf16[64,8,1152]{2,1,0:T(8,128)(2,1)S(1)} %pad_maximum_fusion.1), channel_id=1, replica_groups=mesh['rep'=8,'z'=8,'y'=8] {'z','y'}, dimensions={0} | all-to-all | bytes 2359296 | tf_op jit(solution)/shard_map/all_to_all | solution.py:168
  212.9 1.0 all_gather_reshape.3
  214.2 9.7 %spatial_backward.1 = (bf16[256,1152]{1,0:T(8,128)(2,1)}, f32[3,1152]{1,0:T(4,128)S(1)}) custom-call(bf16[256,1152]{1,0:T(8,128)(2,1)S(1)} %reshape.340.g, bf16[256,1152]{1,0:T(8,128)(2,1)S(1)} %bitcast.58, f32[3,1152]{1,0:T(4,128)S(1)} %copy-done.2, bf16[1152,2432]{1,0:T(8,128)(2,1)} %all-gather.12.cloned.1.call-done.full, s32[256,1]{1,0:T(8,128)S(1)} %select_n.96.lab_k, ...), custom_call_target="tpu_custom_call" | custom-call | flops 6000000000 | bytes 8000000 | tf_op jit(solution)/shard_map/spatial_backward/pallas_call | solution.py:312
  224.0 0.7 broadcast_in_dim.37
  224.7 4.9 %all-to-all-start.4 = ((f32[8,8,864]{2,1,0:T(8,128)}), f32[8,8,864]{2,1,0:T(8,128)S(1)}, u32[]{:S(2)}, u32[]{:S(2)}) async-start(f32[8,8,864]{2,1,0:T(8,128)} %broadcast_in_dim.37), calls=%async_computation.4 | async-start | bytes 458752 | tf_op jit(solution)/shard_map/all_to_all | solution.py:168
  229.8 8.9 %all-to-all-done.4 = f32[8,8,864]{2,1,0:T(8,128)S(1)} async-done(((f32[8,8,864]{2,1,0:T(8,128)}), f32[8,8,864]{2,1,0:T(8,128)S(1)}, u32[]{:S(2)}, u32[]{:S(2)}) %all-to-all-start.4) | async-done | bytes 221216 | tf_op jit(solution)/shard_map/all_to_all | solution.py:168
  238.7 0.7 broadcast_in_dim.38
  239.4 3.7 %all-to-all-start.5 = ((f32[8,8,864]{2,1,0:T(8,128)}), f32[8,8,864]{2,1,0:T(8,128)S(1)}, u32[]{:S(2)}, u32[]{:S(2)}) async-start(f32[8,8,864]{2,1,0:T(8,128)} %broadcast_in_dim.38), calls=%async_computation.5 | async-start | bytes 458752 | tf_op jit(solution)/shard_map/all_to_all | solution.py:168
  243.4 8.7 %all-to-all-done.5 = f32[8,8,864]{2,1,0:T(8,128)S(1)} async-done(((f32[8,8,864]{2,1,0:T(8,128)}), f32[8,8,864]{2,1,0:T(8,128)S(1)}, u32[]{:S(2)}, u32[]{:S(2)}) %all-to-all-start.5) | async-done | bytes 221216 | tf_op jit(solution)/shard_map/all_to_all | solution.py:168
  252.9 8.0 %all-to-all-start.6 = ((f32[8,8,864]{2,1,0:T(8,128)}), f32[8,8,864]{2,1,0:T(8,128)S(1)}, u32[]{:S(2)}, u32[]{:S(2)}) async-start(f32[8,8,864]{2,1,0:T(8,128)} %broadcast_in_dim.39), calls=%async_computation.6 | async-start | bytes 458752 | tf_op jit(solution)/shard_map/all_to_all | solution.py:168
  272.6 1.2 dynamic-slice_bitcast_fusion.3
  273.8 0.9 pad_maximum_fusion.4
  (110 shorter events, 15.4 us)
Async XLA Ops:
  7.2 55.2 %all-gather.10.cloned.1.call-start = ((), (), s32[]{:S(2)}) async-start(), calls=%async_computation.8 | async-start | bytes 5640192 | tf_op jit(solution)/shard_map/all_gather | solution.py:222
  11.4 103.9 %all-gather.12.cloned.1.call-start = ((), (), s32[]{:S(2)}) async-start(), calls=%async_computation.9 | async-start | bytes 6303744 | tf_op jit(solution)/shard_map/all_gather | solution.py:192
  52.6 1.3 copy-start.7
  53.8 100.5 %all-gather.14.cloned.1.call-start = ((), (), s32[]{:S(2)}) async-start(), calls=%async_computation.10 | async-start | bytes 6303744 | tf_op jit(solution)/shard_map/all_gather | solution.py:192
  63.1 69.9 %copy-start.5 = (s32[8,1,128]{2,1,0:T(1,128)}, s32[8,1,128]{2,1,0:T(1,128)S(1)}, u32[]{:S(2)}) copy-start(s32[8,1,128]{2,1,0:T(1,128)S(1)} %slice_convert_fusion) | copy-start | bytes 12292
  113.7 1.6 copy-start
  113.7 1.6 copy-start.2
  122.8 12.4 %copy-start.3 = (bf16[3,576,256]{2,1,0:T(8,128)(2,1)}, bf16[3,576,256]{2,1,0:T(8,128)(2,1)S(1)}, u32[]{:S(2)}) copy-start(bf16[3,576,256]{2,1,0:T(8,128)(2,1)S(1)} %get-tuple-element.13.qkv) | copy-start | bytes 2654212
  123.9 25.3 %all-to-all-start.2 = ((bf16[64,4,1152]{2,1,0:T(4,128)(2,1)}), bf16[64,4,1152]{2,1,0:T(4,128)(2,1)}, u32[]{:S(2)}, u32[]{:S(2)}) async-start(bf16[64,4,1152]{2,1,0:T(4,128)(2,1)} %reshape.332), calls=%async_computation.2 | async-start | bytes 1179648 | tf_op jit(solution)/shard_map/all_to_all | solution.py:168
  132.8 139.9 %all-gather.8.cloned.1.call-start = ((), (), s32[]{:S(2)}) async-start(), calls=%async_computation.7 | async-start | bytes 5308416 | tf_op jit(solution)/shard_map/all_gather | solution.py:305
  135.2 19.1 %copy-start.1 = (f32[3,1152]{1,0:T(4,128)S(1)}, f32[3,1152]{1,0:T(4,128)}, u32[]{:S(2)}) copy-start(f32[3,1152]{1,0:T(4,128)} %gains.4) | copy-start | bytes 41476
  212.9 1.4 copy-start.4
  214.2 15.4 %copy-start.6 = (s32[8,1,128]{2,1,0:T(1,128)S(1)}, s32[8,1,128]{2,1,0:T(1,128)}, u32[]{:S(2)}) copy-start(s32[8,1,128]{2,1,0:T(1,128)} %copy-done.5) | copy-start | bytes 12292
  224.7 13.9 %all-to-all-start.4 = ((f32[8,8,864]{2,1,0:T(8,128)}), f32[8,8,864]{2,1,0:T(8,128)S(1)}, u32[]{:S(2)}, u32[]{:S(2)}) async-start(f32[8,8,864]{2,1,0:T(8,128)} %broadcast_in_dim.37), calls=%async_computation.4 | async-start | bytes 458752 | tf_op jit(solution)/shard_map/all_to_all | solution.py:168
  239.4 12.8 %all-to-all-start.5 = ((f32[8,8,864]{2,1,0:T(8,128)}), f32[8,8,864]{2,1,0:T(8,128)S(1)}, u32[]{:S(2)}, u32[]{:S(2)}) async-start(f32[8,8,864]{2,1,0:T(8,128)} %broadcast_in_dim.38), calls=%async_computation.5 | async-start | bytes 458752 | tf_op jit(solution)/shard_map/all_to_all | solution.py:168
  252.9 19.0 %all-to-all-start.6 = ((f32[8,8,864]{2,1,0:T(8,128)}), f32[8,8,864]{2,1,0:T(8,128)S(1)}, u32[]{:S(2)}, u32[]{:S(2)}) async-start(f32[8,8,864]{2,1,0:T(8,128)} %broadcast_in_dim.39), calls=%async_computation.6 | async-start | bytes 458752 | tf_op jit(solution)/shard_map/all_to_all | solution.py:168
Sparse Core Ops, SparseCore 0:
  11.5 46.8 all-gather.9
  60.5 43.3 all-gather.11
  114.8 39.4 all-gather.13
  214.0 36.1 all-gather.7
where the time goes:
time: 283 us; the launch traced here: 281 us
  blocking collectives  122 us (43%)
  between operations  34.4 us (12%)
  waiting for transfers between devices  33.9 us (12%)
  Pallas kernels  30.8 us (11%)
  starting transfers between devices  25.8 us (9%)
  local copies, waits for them, and re-layouts  23.2 us (8%)
  other arithmetic  10.7 us (4%)
    all_to_all x3, blocking collectives, exchange(): return lax.all_to_all(rows, axes, split_axis=0, concat_axis=0, tiled=True)  122 us
    all_to_all x4, waiting for transfers between devices, exchange(): return lax.all_to_all(rows, axes, split_axis=0, concat_axis=0, tiled=True)  30.2 us
    all_to_all x4, starting transfers between devices, exchange(): return lax.all_to_all(rows, axes, split_axis=0, concat_axis=0, tiled=True)  25.5 us
    pallas_call x1, Pallas kernels, local(): call_kernel(temporal_kernel, (ROWS_OUT, ROWS_OUT, GAIN_OUT), True, 'tempo...  13.6 us
    pallas_call x1, Pallas kernels, local(): call_kernel(spatial_backward_kernel, (ROWS_OUT, GAIN_OUT), True, 'spatial...  9.69 us
    pallas_call x1, Pallas kernels, local(): call_kernel(spatial_forward_kernel, (ROWS_OUT, QKV_OUT), False, 'spatial_...  7.51 us
  transfers between devices with their start and end apart: 8, of which 4 were waited for; matrix products, arithmetic and copies ran while one was open for 9% of the time, Pallas kernels for 6%

commit v1 on v0

--- a/solution.py
+++ b/solution.py
@@ -42,7 +42,7 @@
         u_ref[72 * part : 72 * part + 72, U_CUT:] = block[72:, : 1152 - U_CUT]
 
 
-def forward(v_ref, gains_ref, full_ref, key_label, query_label, out_ref, q_ref, k_ref, x_ref, o_ref, u_ref):
+def forward(v_ref, gains_ref, full_ref, key_label, query_label, q_ref, k_ref, x_ref, o_ref):
     normed, scale = normed_of(v_ref)
 
     def project(which, first, past):
@@ -61,7 +61,10 @@
         o_ref[rows, :] = jnp.dot(
             vals, weights.astype(jnp.bfloat16), preferred_element_type=jnp.float32
         )
-    mixed = jnp.transpose(o_ref[...]).astype(jnp.bfloat16)
+    return jnp.transpose(o_ref[...]).astype(jnp.bfloat16)
+
+
+def finish(v_ref, mixed, u_ref, out_ref):
     made = jnp.dot(mixed, u_ref[...].astype(jnp.bfloat16), preferred_element_type=jnp.float32)
     out_ref[...] = (v_ref[...].astype(jnp.float32) + made).astype(jnp.bfloat16)
 
@@ -119,7 +122,7 @@
 
 def spatial_forward_kernel(v, gains, full, lab_k, lab_q, mid, qkv, q, k, x, o, u):
     load_u(full, u)
-    forward(v, gains, full, lab_k[...], lab_q[...], mid, q, k, x, o, u)
+    finish(v, forward(v, gains, full, lab_k[...], lab_q[...], q, k, x, o), u, mid)
     for which, ref in enumerate((q, k, x)):
         qkv[which] = ref[...].astype(jnp.bfloat16)
 
@@ -134,17 +137,24 @@
 
 
 def temporal_kernel(
-    g, v, gains, full, lab_k, lab_q, out, grad, gain, q, k, x, o, u, dq, dk, dx
+    g, v, gains, full, lab_k, lab_q, mixed, grad, gain, q, k, x, o, u, dq, dk, dx
 ):
     load_u(full, u)
-    forward(v, gains, full, lab_k[...], lab_q[...], out, q, k, x, o, u)
+    mixed[...] = forward(v, gains, full, lab_k[...], lab_q[...], q, k, x, o)
     backward(g, v, gains, full, lab_k[...], lab_q[...], grad, gain, q, k, x, o, u, dq, dk, dx)
+
+
+def finish_kernel(v, mixed, full, out, u):
+    load_u(full, u)
+    finish(v, mixed[...], u, out)
 
 
 def call_kernel(kernel, outs, backs, name):
     rows = 256
     wide = pltpu.VMEM((INNER, rows), jnp.float32)
     scratch = [wide] * 4 + [pltpu.VMEM((INNER, 1152), jnp.float32)]
+    if kernel is finish_kernel:
+        scratch = scratch[4:]
     if backs:
         scratch += [pltpu.VMEM((640, rows), jnp.float32)] * 3
     return pl.pallas_call(
@@ -160,6 +170,7 @@
 
 
 ROWS_OUT = jax.ShapeDtypeStruct((256, 1152), jnp.bfloat16)
+MIXED_OUT = jax.ShapeDtypeStruct((256, 576), jnp.bfloat16)
 GAIN_OUT = jax.ShapeDtypeStruct((3, 1152), jnp.float32)
 QKV_OUT = jax.ShapeDtypeStruct((3, 576, 256), jnp.bfloat16)
 
@@ -216,72 +227,64 @@
     rows = bins_here * slots
     sizes = (qkv_spatial.shape[1], proj_spatial.shape[1], width // groups, inner // groups)
 
-    mine = jnp.concatenate([destination, token_counts[:, 0], frame_counts.reshape(-1)])
-    mine = jnp.pad(mine.astype(jnp.bfloat16)[None], ((0, 15), (0, width - mine.shape[0])))
-    sent = jnp.concatenate([cotangent.reshape(rows, width), mine], axis=0)
+    mine = jnp.pad(destination.astype(jnp.bfloat16)[None], ((0, 15), (0, width - bins_here)))
+    sent = jnp.concatenate([latents.reshape(rows, width), mine], axis=0)
     shared = lax.all_gather(sent, "rep", axis=0, tiled=False)
 
     flat_s = own_piece(qkv_spatial, proj_spatial, group, groups)
     flat_s = jnp.pad(flat_s, (0, -flat_s.shape[0] % 256))
-    got_s = spread(flat_s.reshape(2, -1), SEQ).reshape(frames, -1)
-    full_s = gather_weights(got_s, *sizes)
-
-    facts = shared[:, rows, :128].astype(jnp.int32)
-    dest_all = facts[:, :bins_here]
-    tokens_all = facts[:, bins_here : 2 * bins_here].reshape(-1)
-    videos_all = facts[:, 2 * bins_here : 2 * bins_here + frame_counts.size]
-    videos_all = videos_all.reshape(groups * bins_here, -1)
-    group_ids = jnp.arange(groups, dtype=jnp.int32)
-    bin_ids = jnp.arange(bins_here, dtype=jnp.int32)
-    earlier = (dest_all[None] == destination[:, None, None]) & (
-        group_ids[None, :, None] < group
-    )
-    rank = jnp.sum(earlier.astype(jnp.int32), axis=(1, 2))
-    new_place = destination * bins_here + rank
-    pick_new = (new_place[:, None] == jnp.arange(groups * bins_here, dtype=jnp.int32)).astype(
-        jnp.int32
-    )
-    my_tokens = jnp.sum(pick_new * tokens_all[None], axis=1)
-    my_videos = jnp.sum(pick_new[:, :, None] * videos_all[None], axis=1)
-    comes = jnp.any(dest_all == group, axis=1).astype(jnp.int32)
-    order = jnp.cumsum(comes) - 1
-    source = ((order[None] == bin_ids[:, None]) & (comes[None] > 0)).astype(jnp.int32)
-    from_group = jnp.sum(source * group_ids[None], axis=1)
-    bin_there = jnp.sum((dest_all == group).astype(jnp.int32) * bin_ids[None], axis=1)
-    from_bin = jnp.sum(source * bin_there[None], axis=1)
-
-    cot_here = jnp.stack(
-        [
-            lax.dynamic_slice(shared, (destination[i], rank[i] * slots, 0), (1, slots, width))[0]
-            for i in range(bins_here)
-        ]
-    )
+    got_s = spread(flat_s.reshape(2, -1), SEQ)
+
     flat_t = own_piece(qkv_temporal, proj_temporal, group, groups).reshape(tokens, -1)
     flat_t = jnp.pad(flat_t, ((0, 0), (0, -flat_t.shape[1] % 128)))
     mixed = jnp.concatenate(
         [
-            cot_here.reshape(frames, tokens, width),
+            cotangent.reshape(frames, tokens, width),
             jnp.broadcast_to(flat_t[None], (frames,) + flat_t.shape),
         ],
         axis=2,
     )
+    got_s, mixed = lax.optimization_barrier((got_s, mixed))
+    full_s = gather_weights(got_s.reshape(frames, -1), *sizes)
     mixed = exchange(mixed, SEQ)
-    cot_tokens = mixed[:, :, :width].reshape(rows, width)
     piece = sizes[0] * sizes[2] + sizes[1] * sizes[3]
     full_t = gather_weights(
         mixed[:, :, width : width + piece // tokens].reshape(frames, -1), *sizes
     )
-
-    key_ok = jnp.arange(slots, dtype=jnp.int32)[None, :] < my_tokens[:, None]
+    cot_tokens = mixed[:, :, :width].reshape(rows, width)
+
+    dest_all = shared[:, rows, :bins_here].astype(jnp.int32)
+    group_ids = jnp.arange(groups, dtype=jnp.int32)
+    bin_ids = jnp.arange(bins_here, dtype=jnp.int32)
+    here = (dest_all == group).astype(jnp.int32)
+    comes = jnp.sum(here, axis=1)
+    order = jnp.sum((group_ids[None] < group_ids[:, None]).astype(jnp.int32) * comes[None], axis=1)
+    source = (order[None] == bin_ids[:, None]).astype(jnp.int32) * comes[None]
+    from_group = jnp.sum(source * group_ids[None], axis=1)
+    from_bin = jnp.sum(source * jnp.sum(here * bin_ids[None], axis=1)[None], axis=1)
+    earlier = (dest_all[None] == destination[:, None, None]) & (group_ids[None, :, None] < group)
+    rank = jnp.sum(earlier.astype(jnp.int32), axis=(1, 2))
+
+    def pick(everyone, groups_of, bins_of):
+        return jnp.concatenate(
+            [
+                lax.dynamic_slice(
+                    everyone, (groups_of[i], bins_of[i] * slots, 0), (1, slots, width)
+                )[0]
+                for i in range(bins_here)
+            ]
+        )
+
+    moved = pick(shared, from_group, from_bin)
+    key_ok = jnp.arange(slots, dtype=jnp.int32)[None, :] < token_counts
     lab_k = jnp.where(key_ok, bin_ids[:, None], -1).reshape(rows, 1)
     lab_q = jnp.broadcast_to(bin_ids[:, None], (bins_here, slots)).reshape(1, rows)
-    values = latents.reshape(rows, width)
     mid, qkv = call_kernel(spatial_forward_kernel, (ROWS_OUT, QKV_OUT), False, "spatial_forward")(
-        values, gains_spatial, full_s, lab_k, lab_q
+        moved, gains_spatial, full_s, lab_k, lab_q
     )
     mid_tokens = exchange(mid.reshape(frames, tokens, width), SEQ).reshape(rows, width)
 
-    ends = jnp.cumsum(my_videos, axis=1)
+    ends = jnp.cumsum(frame_counts, axis=1)
     video_id = jnp.sum(
         (ends[:, None, :] <= jnp.arange(frames, dtype=jnp.int32)[None, :, None]).astype(jnp.int32),
         axis=2,
@@ -289,34 +292,25 @@
     row_bin = place * tokens // slots
     video_row = jnp.sum((bin_ids == row_bin).astype(jnp.int32)[:, None] * video_id, axis=0)
     lab_t = video_row[:, None] * tokens + jnp.arange(tokens, dtype=jnp.int32)[None]
-    out_tokens, mid_grad_tokens, grad_temporal = call_kernel(
-        temporal_kernel, (ROWS_OUT, ROWS_OUT, GAIN_OUT), True, "temporal"
+    heads_tokens, mid_grad_tokens, grad_temporal = call_kernel(
+        temporal_kernel, (MIXED_OUT, ROWS_OUT, GAIN_OUT), True, "temporal"
     )(cot_tokens, mid_tokens, gains_temporal, full_t, lab_t.reshape(rows, 1), lab_t.reshape(1, rows))
 
-    both = jnp.concatenate(
-        [
-            mid_grad_tokens.reshape(frames, tokens, width),
-            out_tokens.reshape(frames, tokens, width),
-        ],
-        axis=1,
-    )
-    both = exchange(both, SEQ)
-    mid_grad = both[:, :tokens].reshape(rows, width)
-    outs = lax.all_gather(both[:, tokens:].reshape(rows, width), "rep", axis=0, tiled=False)
-    block_out = jnp.stack(
-        [
-            lax.dynamic_slice(outs, (from_group[j], from_bin[j] * slots, 0), (1, slots, width))
-            for j in range(bins_here)
-        ]
-    )
-    latent_grad, grad_spatial = call_kernel(
+    both = jnp.concatenate([mid_grad_tokens, heads_tokens], axis=1)
+    both = exchange(both.reshape(frames, tokens, width + inner), SEQ)
+    both = both.reshape(rows, width + inner)
+    mid_grad, heads_here = both[:, :width], both[:, width:]
+    moved_grad, grad_spatial = call_kernel(
         spatial_backward_kernel, (ROWS_OUT, GAIN_OUT), True, "spatial_backward"
-    )(mid_grad, values, gains_spatial, full_s, lab_k, lab_q, qkv)
+    )(mid_grad, moved, gains_spatial, full_s, lab_k, lab_q, qkv)
+    block_out = call_kernel(finish_kernel, ROWS_OUT, False, "finish")(mid, heads_here, full_t)
+    returned = lax.all_gather(moved_grad, "rep", axis=0, tiled=False)
+    latent_grad = pick(returned, destination, rank)
     sums = jnp.stack([grad_spatial, grad_temporal]).reshape(8, -1)
     for axis in ("y", "z", "rep"):
         sums = jnp.sum(spread(sums, axis), axis=0)
     gain_grads = sums.reshape((2,) + gains_spatial.shape)
-    return (block_out, latent_grad.reshape(latents.shape), gain_grads)
+    return (block_out.reshape(latents.shape), latent_grad.reshape(latents.shape), gain_grads)
 
 
 def solution(mesh):

time: 283 us -> 264 us (0.933)
  blocking collectives: 122 us -> 77.2 us
  starting transfers between devices: 25.8 us -> 42.9 us
  waiting for transfers between devices: 33.9 us -> 43.4 us
  Pallas kernels: 30.8 us -> 34 us
    all_to_all x3 -> x2, blocking collectives: 122 us -> 77.2 us  [exchange(): return lax.all_to_all(rows, axes, split_axis=0, concat_axis=0, tiled=True)]
    all_to_all x4 -> x5, starting transfers between devices: 25.5 us -> 42.5 us  [exchange(): return lax.all_to_all(rows, axes, split_axis=0, concat_axis=0, tiled=True)]
    all_to_all x4 -> x5, waiting for transfers between devices: 30.2 us -> 40.2 us  [exchange(): return lax.all_to_all(rows, axes, split_axis=0, concat_axis=0, tiled=True)]
    pallas_call x1 -> x2, Pallas kernels: 13.6 us -> 16.9 us  [the longest x1 12.8 us: local(): call_kernel(temporal_kernel, (MIXED_OUT, ROWS_OUT, GAIN_OUT), True, 'temp...]
  transfers between devices with their start and end apart: 8 -> 9, of which waited for: 4 -> 6; matrix products, arithmetic and copies ran while one was open for 9% -> 9% of each run, Pallas kernels for 6% -> 4%
where the time goes in v1:
time: 264 us; the launch traced here: 263 us
  blocking collectives  77.2 us (29%)
  waiting for transfers between devices  43.4 us (16%)
  starting transfers between devices  42.9 us (16%)
  between operations  34.2 us (13%)
  Pallas kernels  34 us (13%)
  local copies, waits for them, and re-layouts  23.4 us (9%)
  other arithmetic  7.88 us (3%)
    all_to_all x2, blocking collectives, exchange(): return lax.all_to_all(rows, axes, split_axis=0, concat_axis=0, tiled=True)  77.2 us
    all_to_all x5, starting transfers between devices, exchange(): return lax.all_to_all(rows, axes, split_axis=0, concat_axis=0, tiled=True)  42.5 us
    all_to_all x5, waiting for transfers between devices, exchange(): return lax.all_to_all(rows, axes, split_axis=0, concat_axis=0, tiled=True)  40.2 us
    pallas_call x1, Pallas kernels, local(): call_kernel(temporal_kernel, (MIXED_OUT, ROWS_OUT, GAIN_OUT), True, 'temp...  12.8 us
    pallas_call x1, Pallas kernels, local(): call_kernel(spatial_backward_kernel, (ROWS_OUT, GAIN_OUT), True, 'spatial...  9.65 us
    pallas_call x1, Pallas kernels, local(): call_kernel(spatial_forward_kernel, (ROWS_OUT, QKV_OUT), False, 'spatial_...  7.51 us
  transfers between devices with their start and end apart: 9, of which 6 were waited for; matrix products, arithmetic and copies ran while one was open for 9% of the time, Pallas kernels for 4%

profile of v1, /device:TPU:1, one launch (start us, length us, event | category | flops | bytes accessed | tf_op | source)
XLA Modules:
  0.0 263.0 jit_solution(15594199412052426421)
XLA Ops:
  7.9 1.9 fusion.12
  9.8 0.9 dynamic-slice_bitcast_fusion.10
  10.8 0.8 dynamic-slice_bitcast_fusion.8
  11.9 1.2 broadcast_in_dim.34
  13.1 17.1 %all-to-all-start = ((bf16[64,2,2688]{2,1,0:T(2,128)(2,1)}), bf16[64,2,2688]{2,1,0:T(2,128)(2,1)S(1)}, u32[]{:S(2)}, u32[]{:S(2)}) async-start(bf16[64,2,2688]{2,1,0:T(2,128)(2,1)} %broadcast_in_dim.34), calls=%async_computation | async-start | bytes 1376256 | tf_op jit(solution)/shard_map/all_to_all | solution.py:179
  31.6 18.5 %all-to-all-done = bf16[64,2,2688]{2,1,0:T(2,128)(2,1)S(1)} async-done(((bf16[64,2,2688]{2,1,0:T(2,128)(2,1)}), bf16[64,2,2688]{2,1,0:T(2,128)(2,1)S(1)}, u32[]{:S(2)}, u32[]{:S(2)}) %all-to-all-start) | async-done | bytes 688160 | tf_op jit(solution)/shard_map/all_to_all | solution.py:179
  51.0 1.1 reshape.220
  52.4 0.9 fusion.9
  53.4 39.3 %all_to_all.35 = bf16[64,4,2560]{2,1,0:T(4,128)(2,1)S(1)} all-to-all(bf16[64,4,2560]{2,1,0:T(4,128)(2,1)S(1)} %pad_maximum_fusion), channel_id=1, replica_groups=mesh['rep'=8,'z'=8,'y'=8] {'z','y'}, dimensions={0} | all-to-all | bytes 2621440 | tf_op jit(solution)/shard_map/all_to_all | solution.py:179
  92.6 1.1 copy-done.4
  95.3 1.1 reshape.228
  96.7 0.9 fusion.11
  109.5 1.2 dynamic-slice_bitcast_fusion.7
  110.8 7.5 %spatial_forward.1 = (bf16[256,1152]{1,0:T(8,128)(2,1)S(1)}, bf16[3,576,256]{2,1,0:T(8,128)(2,1)S(1)}) custom-call(bf16[256,1152]{1,0:T(8,128)(2,1)S(1)} %pad_maximum_fusion.2.v, f32[3,1152]{1,0:T(4,128)S(1)} %copy-done.1, bf16[1152,2432]{1,0:T(8,128)(2,1)} %all-gather.11.cloned.1.call-done.full, s32[256,1]{1,0:T(8,128)S(1)} %select_n.96.lab_k, ...), custom_call_target="tpu_custom_call" | custom-call | flops 6000000000 | bytes 8000000 | tf_op jit(solution)/shard_map/spatial_forward/pallas_call | solution.py:282
  118.3 1.1 reshape.225
  119.4 8.9 %all-to-all-start.2 = ((bf16[64,4,1152]{2,1,0:T(4,128)(2,1)}), bf16[64,4,1152]{2,1,0:T(4,128)(2,1)S(1)}, u32[]{:S(2)}, u32[]{:S(2)}) async-start(bf16[64,4,1152]{2,1,0:T(4,128)(2,1)} %reshape.225), calls=%async_computation.2 | async-start | bytes 1179648 | tf_op jit(solution)/shard_map/all_to_all | solution.py:179
  129.6 0.8 add.131.lab_k
  130.5 0.9 add.122.lab_q
  131.5 13.3 %all-to-all-done.2 = bf16[64,4,1152]{2,1,0:T(4,128)(2,1)S(1)} async-done(((bf16[64,4,1152]{2,1,0:T(4,128)(2,1)}), bf16[64,4,1152]{2,1,0:T(4,128)(2,1)S(1)}, u32[]{:S(2)}, u32[]{:S(2)}) %all-to-all-start.2) | async-done | bytes 589856 | tf_op jit(solution)/shard_map/all_to_all | solution.py:179
  145.0 3.1 %all-gather.13.cloned.1.call-done.full = bf16[1152,2432]{1,0:T(8,128)(2,1)} async-done(((bf16[144,2432]{1,0:T(8,128)(2,1)}), bf16[1152,2432]{1,0:T(8,128)(2,1)}) %all-gather.13.cloned.1.call-update) | async-done | bytes 5603344 | tf_op jit(solution)/shard_map/all_gather | solution.py:203
  148.1 12.8 %temporal.1 = (bf16[256,576]{1,0:T(8,128)(2,1)S(1)}, bf16[256,1152]{1,0:T(8,128)(2,1)S(1)}, f32[3,1152]{1,0:T(4,128)S(1)}) custom-call(bf16[256,1152]{1,0:T(8,128)(2,1)S(1)} %reshape.224.g, bf16[256,1152]{1,0:T(8,128)(2,1)S(1)} %reshape.226.v, f32[3,1152]{1,0:T(4,128)S(1)} %copy-done, bf16[1152,2432]{1,0:T(8,128)(2,1)} %all-gather.13.cloned.1.call-done.full, ...), custom_call_target="tpu_custom_call" | custom-call | flops 6000000000 | bytes 8000000 | tf_op jit(solution)/shard_map/temporal/pallas_call | solution.py:295
  161.3 37.9 %all_to_all.36 = bf16[64,4,1728]{2,1,0:T(4,128)(2,1)} all-to-all(bf16[64,4,1728]{2,1,0:T(4,128)(2,1)S(1)} %reshape.231), channel_id=1, replica_groups=mesh['rep'=8,'z'=8,'y'=8] {'z','y'}, dimensions={0} | all-to-all | bytes 1769472 | tf_op jit(solution)/shard_map/all_to_all | solution.py:179
  199.2 1.7 reshape.232
  201.0 9.7 %spatial_backward.1 = (bf16[256,1152]{1,0:T(8,128)(2,1)}, f32[3,1152]{1,0:T(4,128)S(1)}) custom-call(bf16[256,1152]{1,0:T(8,128)(2,1)S(1)} %slice.128.g, bf16[256,1152]{1,0:T(8,128)(2,1)S(1)} %pad_maximum_fusion.2.v, f32[3,1152]{1,0:T(4,128)S(1)} %copy-done.1, bf16[1152,2432]{1,0:T(8,128)(2,1)} %all-gather.11.cloned.1.call-done.full, ...), custom_call_target="tpu_custom_call" | custom-call | flops 6000000000 | bytes 8000000 | tf_op jit(solution)/shard_map/spatial_backward/pallas_call | solution.py:303
  211.5 5.2 %all-to-all-start.4 = ((f32[8,8,864]{2,1,0:T(8,128)}), f32[8,8,864]{2,1,0:T(8,128)S(1)}, u32[]{:S(2)}, u32[]{:S(2)}) async-start(f32[8,8,864]{2,1,0:T(8,128)} %broadcast_in_dim.40), calls=%async_computation.4 | async-start | bytes 458752 | tf_op jit(solution)/shard_map/all_to_all | solution.py:179
  226.4 3.4 %all-to-all-start.5 = ((f32[8,8,864]{2,1,0:T(8,128)}), f32[8,8,864]{2,1,0:T(8,128)S(1)}, u32[]{:S(2)}, u32[]{:S(2)}) async-start(f32[8,8,864]{2,1,0:T(8,128)} %broadcast_in_dim.41), calls=%async_computation.5 | async-start | bytes 458752 | tf_op jit(solution)/shard_map/all_to_all | solution.py:179
  233.4 5.5 %all-to-all-done.5 = f32[8,8,864]{2,1,0:T(8,128)S(1)} async-done(((f32[8,8,864]{2,1,0:T(8,128)}), f32[8,8,864]{2,1,0:T(8,128)S(1)}, u32[]{:S(2)}, u32[]{:S(2)}) %all-to-all-start.5) | async-done | bytes 221216 | tf_op jit(solution)/shard_map/all_to_all | solution.py:179
  239.6 7.9 %all-to-all-start.6 = ((f32[8,8,864]{2,1,0:T(8,128)}), f32[8,8,864]{2,1,0:T(8,128)S(1)}, u32[]{:S(2)}, u32[]{:S(2)}) async-start(f32[8,8,864]{2,1,0:T(8,128)} %broadcast_in_dim.42), calls=%async_computation.6 | async-start | bytes 458752 | tf_op jit(solution)/shard_map/all_to_all | solution.py:179
  247.5 4.0 %finish.1 = bf16[256,1152]{1,0:T(8,128)(2,1)} custom-call(bf16[256,1152]{1,0:T(8,128)(2,1)S(1)} %get-tuple-element.13.v, bf16[256,576]{1,0:T(8,128)(2,1)S(1)} %slice.127.mixed, bf16[1152,2432]{1,0:T(8,128)(2,1)} %all-gather.13.cloned.1.call-done.full), custom_call_target="tpu_custom_call" | custom-call | flops 6000000000 | bytes 8000000 | tf_op jit(solution)/shard_map/finish/pallas_call | solution.py:306
  251.5 2.2 all-to-all-done.6
  254.4 1.2 dynamic-slice_bitcast_fusion.3
  255.6 0.9 pad_maximum_fusion.3
  (99 shorter events, 14.9 us)
Async XLA Ops:
  7.2 90.8 %all-gather.9.cloned.1.call-start = ((), (), s32[]{:S(2)}) async-start(), calls=%async_computation.7 | async-start | bytes 5640192 | tf_op jit(solution)/shard_map/all_gather | solution.py:232
  9.8 20.8 %copy-start.5 = (bf16[4,1,64,1152]{3,2,1,0:T(8,128)(2,1)S(1)}, bf16[4,1,64,1152]{3,2,1,0:T(8,128)(2,1)}, u32[]{:S(2)}) copy-start(bf16[4,1,64,1152]{3,2,1,0:T(8,128)(2,1)} %param.21) | copy-start | bytes 1769476
  13.1 37.0 %all-to-all-start = ((bf16[64,2,2688]{2,1,0:T(2,128)(2,1)}), bf16[64,2,2688]{2,1,0:T(2,128)(2,1)S(1)}, u32[]{:S(2)}, u32[]{:S(2)}) async-start(bf16[64,2,2688]{2,1,0:T(2,128)(2,1)} %broadcast_in_dim.34), calls=%async_computation | async-start | bytes 1376256 | tf_op jit(solution)/shard_map/all_to_all | solution.py:179
  30.2 80.5 %all-gather.11.cloned.1.call-start = ((), (), s32[]{:S(2)}) async-start(), calls=%async_computation.8 | async-start | bytes 6303744 | tf_op jit(solution)/shard_map/all_gather | solution.py:203
  53.3 94.8 %all-gather.13.cloned.1.call-start = ((), (), s32[]{:S(2)}) async-start(), calls=%async_computation.9 | async-start | bytes 6303744 | tf_op jit(solution)/shard_map/all_gather | solution.py:203
  92.6 1.1 copy-start.4
  96.4 1.2 copy-start.8
  97.6 13.1 %copy-start.1 = (f32[3,1152]{1,0:T(4,128)S(1)}, f32[3,1152]{1,0:T(4,128)}, u32[]{:S(2)}) copy-start(f32[3,1152]{1,0:T(4,128)} %gains.5) | copy-start | bytes 41476
  118.3 13.1 %copy-start.2 = (bf16[3,576,256]{2,1,0:T(8,128)(2,1)}, bf16[3,576,256]{2,1,0:T(8,128)(2,1)S(1)}, u32[]{:S(2)}) copy-start(bf16[3,576,256]{2,1,0:T(8,128)(2,1)S(1)} %get-tuple-element.17.qkv) | copy-start | bytes 2654212
  118.3 10.3 %copy-start.7 = (s32[4,4]{1,0:T(4,128)S(1)}, s32[4,4]{1,0:T(4,128)}, u32[]{:S(2)}) copy-start(s32[4,4]{1,0:T(4,128)} %param.14) | copy-start | bytes 196
  119.4 12.0 %slice-start = ((bf16[64,4,2560]{2,1,0:T(4,128)(2,1)}), bf16[64,4,1152]{2,1,0:T(4,128)(2,1)S(1)}, s32[]{:S(2)}) async-start(bf16[64,4,2560]{2,1,0:T(4,128)(2,1)} %copy-done.4), calls=%async_computation.11 | async-start | bytes 1179648 | tf_op jit(solution)/shard_map/slice | solution.py:254
  119.4 25.5 %all-to-all-start.2 = ((bf16[64,4,1152]{2,1,0:T(4,128)(2,1)}), bf16[64,4,1152]{2,1,0:T(4,128)(2,1)S(1)}, u32[]{:S(2)}, u32[]{:S(2)}) async-start(bf16[64,4,1152]{2,1,0:T(4,128)(2,1)} %reshape.225), calls=%async_computation.2 | async-start | bytes 1179648 | tf_op jit(solution)/shard_map/all_to_all | solution.py:179
  128.3 126.2 %all-gather.15.cloned.1.call-start = ((), (), s32[]{:S(2)}) async-start(), calls=%async_computation.10 | async-start | bytes 5308416 | tf_op jit(solution)/shard_map/all_gather | solution.py:307
  131.4 16.7 %copy-start = (f32[3,1152]{1,0:T(4,128)S(1)}, f32[3,1152]{1,0:T(4,128)}, u32[]{:S(2)}) copy-start(f32[3,1152]{1,0:T(4,128)} %gains.4) | copy-start | bytes 41476
  199.2 1.8 copy-start.3
  210.6 6.0 %copy-start.6 = (s32[4]{0:T(128)S(1)}, s32[4]{0:T(128)}, u32[]{:S(2)}) copy-start(s32[4]{0:T(128)} %param.12) | copy-start | bytes 52
  211.5 14.2 %all-to-all-start.4 = ((f32[8,8,864]{2,1,0:T(8,128)}), f32[8,8,864]{2,1,0:T(8,128)S(1)}, u32[]{:S(2)}, u32[]{:S(2)}) async-start(f32[8,8,864]{2,1,0:T(8,128)} %broadcast_in_dim.40), calls=%async_computation.4 | async-start | bytes 458752 | tf_op jit(solution)/shard_map/all_to_all | solution.py:179
  226.4 12.4 %all-to-all-start.5 = ((f32[8,8,864]{2,1,0:T(8,128)}), f32[8,8,864]{2,1,0:T(8,128)S(1)}, u32[]{:S(2)}, u32[]{:S(2)}) async-start(f32[8,8,864]{2,1,0:T(8,128)} %broadcast_in_dim.41), calls=%async_computation.5 | async-start | bytes 458752 | tf_op jit(solution)/shard_map/all_to_all | solution.py:179
  239.6 14.1 %all-to-all-start.6 = ((f32[8,8,864]{2,1,0:T(8,128)}), f32[8,8,864]{2,1,0:T(8,128)S(1)}, u32[]{:S(2)}, u32[]{:S(2)}) async-start(f32[8,8,864]{2,1,0:T(8,128)} %broadcast_in_dim.42), calls=%async_computation.6 | async-start | bytes 458752 | tf_op jit(solution)/shard_map/all_to_all | solution.py:179
Sparse Core Ops, SparseCore 0:
  10.1 46.7 all-gather.8
  59.0 43.3 all-gather.10
  104.6 43.4 all-gather.12
  210.8 35.5 all-gather.14

commit v2 on v1

--- a/solution.py
+++ b/solution.py
@@ -12,8 +12,8 @@
 HD = 72
 INNER = HEADS * HD
 SEQ = ("z", "y")
-W_PAD = 1792
-U_CUT = 640
+CUTS = (0, 640, 1152, 1792, 2304)
+U_FROM = 1664
 
 
 def scores_of(q_ref, k_ref, head, allowed):
@@ -35,17 +35,31 @@
     return wide * scale, scale
 
 
+def weight_copies(full_hbm, full_ref, sems):
+    return [
+        pltpu.make_async_copy(
+            full_hbm.at[:, CUTS[i] : CUTS[i + 1]], full_ref.at[:, CUTS[i] : CUTS[i + 1]], sems.at[i]
+        )
+        for i in range(4)
+    ]
+
+
 def load_u(full_ref, u_ref):
+    lane = lax.broadcasted_iota(jnp.int32, (72, 128), 1)
     for part in range(8):
-        block = full_ref[144 * part : 144 * part + 144, W_PAD : W_PAD + U_CUT].astype(jnp.float32)
-        u_ref[72 * part : 72 * part + 72, :U_CUT] = block[:72]
-        u_ref[72 * part : 72 * part + 72, U_CUT:] = block[72:, : 1152 - U_CUT]
-
-
-def forward(v_ref, gains_ref, full_ref, key_label, query_label, q_ref, k_ref, x_ref, o_ref):
+        rows = slice(72 * part, 72 * part + 72)
+        block = full_ref[144 * part : 144 * part + 144, U_FROM:].astype(jnp.float32)
+        left, right = pltpu.roll(block[:72], 576, 1), block[72:]
+        u_ref[rows, :512] = left[:, :512]
+        u_ref[rows, 512:640] = jnp.where(lane < 64, left[:, 512:], right[:, :128])
+        u_ref[rows, 640:] = right[:, 128:]
+
+
+def forward(v_ref, gains_ref, full_ref, copies, key_label, query_label, q_ref, k_ref, x_ref, o_ref):
     normed, scale = normed_of(v_ref)
 
     def project(which, first, past):
+        copies[which].wait()
         scaled = (normed * gains_ref[which : which + 1, :]).astype(jnp.bfloat16)
         made = jnp.dot(scaled, full_ref[:, first:past], preferred_element_type=jnp.float32)
         return jnp.transpose(made)
@@ -70,7 +84,7 @@
 
 
 def backward(
-    g_ref, v_ref, gains_ref, full_ref, key_label, query_label, grad_ref, gain_ref,
+    g_ref, v_ref, gains_ref, full_ref, copies, key_label, query_label, grad_ref, gain_ref,
     q_ref, k_ref, x_ref, o_ref, u_ref, dq_ref, dk_ref, dx_ref,
 ):
     grad = g_ref[...]
@@ -106,6 +120,8 @@
             d_out, weights.astype(jnp.bfloat16), over_lanes, preferred_element_type=jnp.float32
         )
     normed, scale = normed_of(v_ref)
+    for copy in copies:
+        copy.wait()
     d_normed = None
     for which, (ref, first) in enumerate(((dq_ref, 0), (dk_ref, 512), (dx_ref, 1152))):
         made = jnp.transpose(ref[...]).astype(jnp.bfloat16)
@@ -120,46 +136,113 @@
     grad_ref[...] = result.astype(jnp.bfloat16)
 
 
-def spatial_forward_kernel(v, gains, full, lab_k, lab_q, mid, qkv, q, k, x, o, u):
+def spatial_forward_kernel(
+    starts, everyone, gains, full_hbm, lab_k, lab_q, moved, mid, qkv,
+    full, sems, u, q, k, x, o, pick_sems,
+):
+    copies = weight_copies(full_hbm, full, sems)
+    picks = [
+        pltpu.make_async_copy(
+            everyone.at[pl.ds(pl.multiple_of(starts[i], 16), 64), :],
+            moved.at[64 * i : 64 * i + 64, :],
+            pick_sems.at[i],
+        )
+        for i in range(4)
+    ]
+    for copy in picks + copies:
+        copy.start()
+    for copy in picks:
+        copy.wait()
+    mixed = forward(moved, gains, full, copies, lab_k[...], lab_q[...], q, k, x, o)
+    copies[3].wait()
     load_u(full, u)
-    finish(v, forward(v, gains, full, lab_k[...], lab_q[...], q, k, x, o), u, mid)
+    finish(moved, mixed, u, mid)
     for which, ref in enumerate((q, k, x)):
         qkv[which] = ref[...].astype(jnp.bfloat16)
 
 
 def spatial_backward_kernel(
-    g, v, gains, full, lab_k, lab_q, qkv, grad, gain, q, k, x, o, u, dq, dk, dx
+    g, v, gains, full_hbm, lab_k, lab_q, qkv, grad, gain,
+    full, sems, u, q, k, x, o, dq, dk, dx,
 ):
-    load_u(full, u)
+    copies = weight_copies(full_hbm, full, sems)
+    for copy in copies[::-1]:
+        copy.start()
     for which, ref in enumerate((q, k, x)):
         ref[...] = qkv[which].astype(jnp.float32)
-    backward(g, v, gains, full, lab_k[...], lab_q[...], grad, gain, q, k, x, o, u, dq, dk, dx)
+    copies[3].wait()
+    copies[2].wait()
+    load_u(full, u)
+    backward(
+        g, v, gains, full, copies[:2], lab_k[...], lab_q[...], grad, gain,
+        q, k, x, o, u, dq, dk, dx,
+    )
 
 
 def temporal_kernel(
-    g, v, gains, full, lab_k, lab_q, mixed, grad, gain, q, k, x, o, u, dq, dk, dx
+    g, v, gains, full_hbm, lab_k, lab_q, mixed, grad, gain,
+    full, sems, u, q, k, x, o, dq, dk, dx,
 ):
+    copies = weight_copies(full_hbm, full, sems)
+    for copy in copies:
+        copy.start()
+    mixed[...] = forward(v, gains, full, copies, lab_k[...], lab_q[...], q, k, x, o)
+    copies[3].wait()
     load_u(full, u)
-    mixed[...] = forward(v, gains, full, lab_k[...], lab_q[...], q, k, x, o)
-    backward(g, v, gains, full, lab_k[...], lab_q[...], grad, gain, q, k, x, o, u, dq, dk, dx)
-
-
-def finish_kernel(v, mixed, full, out, u):
+    backward(
+        g, v, gains, full, [], lab_k[...], lab_q[...], grad, gain, q, k, x, o, u, dq, dk, dx
+    )
+
+
+def finish_kernel(v, mixed, full_hbm, out, full, sems, u):
+    copies = weight_copies(full_hbm, full, sems)[2:]
+    for copy in copies:
+        copy.start()
+    for copy in copies:
+        copy.wait()
     load_u(full, u)
     finish(v, mixed[...], u, out)
 
 
-def call_kernel(kernel, outs, backs, name):
+def pick_kernel(starts, everyone, out, sems):
+    picks = [
+        pltpu.make_async_copy(
+            everyone.at[pl.ds(pl.multiple_of(starts[i], 16), 64), :],
+            out.at[64 * i : 64 * i + 64, :],
+            sems.at[i],
+        )
+        for i in range(4)
+    ]
+    for copy in picks:
+        copy.start()
+    for copy in picks:
+        copy.wait()
+
+
+def call_kernel(kernel, outs, name):
+    vmem = pl.BlockSpec(memory_space=pltpu.VMEM)
+    smem = pl.BlockSpec(memory_space=pltpu.SMEM)
+    hbm = pl.BlockSpec(memory_space=pl.ANY)
     rows = 256
-    wide = pltpu.VMEM((INNER, rows), jnp.float32)
-    scratch = [wide] * 4 + [pltpu.VMEM((INNER, 1152), jnp.float32)]
+    four = pltpu.SemaphoreType.DMA((4,))
+    scratch = [
+        pltpu.VMEM((1152, CUTS[-1]), jnp.bfloat16), four, pltpu.VMEM((INNER, 1152), jnp.float32)
+    ]
+    scratch += [pltpu.VMEM((INNER, rows), jnp.float32)] * 4
     if kernel is finish_kernel:
-        scratch = scratch[4:]
-    if backs:
-        scratch += [pltpu.VMEM((640, rows), jnp.float32)] * 3
+        ins, scratch = [vmem, vmem, hbm], scratch[:3]
+    elif kernel is pick_kernel:
+        ins, scratch = [smem, hbm], [four]
+    elif kernel is spatial_forward_kernel:
+        ins, scratch = [smem, hbm, vmem, hbm, vmem, vmem], scratch + [four]
+    else:
+        ins = [vmem] * 3 + [hbm] + [vmem] * (2 if kernel is temporal_kernel else 3)
+        scratch = scratch + [pltpu.VMEM((640, rows), jnp.float32)] * 3
     return pl.pallas_call(
         kernel,
         out_shape=outs,
+        in_specs=ins,
+        out_specs=hbm if kernel is pick_kernel else jax.tree.map(lambda _: vmem, outs),
         scratch_shapes=scratch,
         compiler_params=pltpu.CompilerParams(vmem_limit_bytes=50 * 1024 * 1024),
         cost_estimate=pl.CostEstimate(
@@ -196,10 +279,9 @@
     cut = shard * rows_w
     part_w = got[:, :cut].reshape(peers * shard, rows_w).T
     part_u = got[:, cut : cut + shard_u * rows_u].reshape(peers * shard_u, rows_u).T
-    part_w = jnp.pad(part_w, ((0, 0), (0, W_PAD - part_w.shape[1])))
-    low, high = part_u[:, :U_CUT], part_u[:, U_CUT:]
-    high = jnp.pad(high, ((0, 0), (0, U_CUT - high.shape[1])))
-    part = jnp.concatenate([part_w, jnp.concatenate([low, high], axis=0)], axis=1)
+    half = part_u.shape[1] // 2
+    part_u = jnp.concatenate([part_u[:, :half], part_u[:, half:]], axis=0)
+    part = jnp.concatenate([part_w, part_u], axis=1)
     full = lax.all_gather(part, "rep", axis=0, tiled=False)
     return full.reshape(full.shape[0] * full.shape[1], full.shape[2])
 
@@ -265,23 +347,14 @@
     earlier = (dest_all[None] == destination[:, None, None]) & (group_ids[None, :, None] < group)
     rank = jnp.sum(earlier.astype(jnp.int32), axis=(1, 2))
 
-    def pick(everyone, groups_of, bins_of):
-        return jnp.concatenate(
-            [
-                lax.dynamic_slice(
-                    everyone, (groups_of[i], bins_of[i] * slots, 0), (1, slots, width)
-                )[0]
-                for i in range(bins_here)
-            ]
-        )
-
-    moved = pick(shared, from_group, from_bin)
+    starts_here = from_group * shared.shape[1] + from_bin * slots
+    starts_back = destination * rows + rank * slots
     key_ok = jnp.arange(slots, dtype=jnp.int32)[None, :] < token_counts
     lab_k = jnp.where(key_ok, bin_ids[:, None], -1).reshape(rows, 1)
     lab_q = jnp.broadcast_to(bin_ids[:, None], (bins_here, slots)).reshape(1, rows)
-    mid, qkv = call_kernel(spatial_forward_kernel, (ROWS_OUT, QKV_OUT), False, "spatial_forward")(
-        moved, gains_spatial, full_s, lab_k, lab_q
-    )
+    moved, mid, qkv = call_kernel(
+        spatial_forward_kernel, (ROWS_OUT, ROWS_OUT, QKV_OUT), "spatial_forward"
+    )(starts_here, shared.reshape(-1, width), gains_spatial, full_s, lab_k, lab_q)
     mid_tokens = exchange(mid.reshape(frames, tokens, width), SEQ).reshape(rows, width)
 
     ends = jnp.cumsum(frame_counts, axis=1)
@@ -293,7 +366,7 @@
     video_row = jnp.sum((bin_ids == row_bin).astype(jnp.int32)[:, None] * video_id, axis=0)
     lab_t = video_row[:, None] * tokens + jnp.arange(tokens, dtype=jnp.int32)[None]
     heads_tokens, mid_grad_tokens, grad_temporal = call_kernel(
-        temporal_kernel, (MIXED_OUT, ROWS_OUT, GAIN_OUT), True, "temporal"
+        temporal_kernel, (MIXED_OUT, ROWS_OUT, GAIN_OUT), "temporal"
     )(cot_tokens, mid_tokens, gains_temporal, full_t, lab_t.reshape(rows, 1), lab_t.reshape(1, rows))
 
     both = jnp.concatenate([mid_grad_tokens, heads_tokens], axis=1)
@@ -301,11 +374,13 @@
     both = both.reshape(rows, width + inner)
     mid_grad, heads_here = both[:, :width], both[:, width:]
     moved_grad, grad_spatial = call_kernel(
-        spatial_backward_kernel, (ROWS_OUT, GAIN_OUT), True, "spatial_backward"
+        spatial_backward_kernel, (ROWS_OUT, GAIN_OUT), "spatial_backward"
     )(mid_grad, moved, gains_spatial, full_s, lab_k, lab_q, qkv)
-    block_out = call_kernel(finish_kernel, ROWS_OUT, False, "finish")(mid, heads_here, full_t)
+    block_out = call_kernel(finish_kernel, ROWS_OUT, "finish")(mid, heads_here, full_t)
     returned = lax.all_gather(moved_grad, "rep", axis=0, tiled=False)
-    latent_grad = pick(returned, destination, rank)
+    latent_grad = call_kernel(pick_kernel, ROWS_OUT, "pick")(
+        starts_back, returned.reshape(-1, width)
+    )
     sums = jnp.stack([grad_spatial, grad_temporal]).reshape(8, -1)
     for axis in ("y", "z", "rep"):
         sums = jnp.sum(spread(sums, axis), axis=0)

time: 264 us -> 279 us (1.057)
  between operations: 34.2 us -> 14.2 us
  Pallas kernels: 34 us -> 53.9 us
  waiting for transfers between devices: 43.4 us -> 59.1 us
  starting transfers between devices: 42.9 us -> 47.4 us
  local copies, waits for them, and re-layouts: 23.4 us -> 19.9 us
    pallas_call x4 -> x5, Pallas kernels: 34 us -> 53.9 us  [the longest x1 19.5 us: local(): call_kernel(pick_kernel, ROWS_OUT, 'pick')]
    all_to_all x5, waiting for transfers between devices: 40.2 us -> 56.5 us  [exchange(): return lax.all_to_all(rows, axes, split_axis=0, concat_axis=0, tiled=True)]
    all_to_all x5, starting transfers between devices: 42.5 us -> 47 us  [exchange(): return lax.all_to_all(rows, axes, split_axis=0, concat_axis=0, tiled=True)]
  transfers between devices with their start and end apart: 9 -> 9, of which waited for: 6 -> 7; matrix products, arithmetic and copies ran while one was open for 9% -> 7% of each run, Pallas kernels for 4% -> 5%
where the time goes in v2:
time: 279 us; the launch traced here: 278 us
  blocking collectives  77.4 us (28%)
  waiting for transfers between devices  59.1 us (21%)
  Pallas kernels  53.9 us (19%)
  starting transfers between devices  47.4 us (17%)
  local copies, waits for them, and re-layouts  19.9 us (7%)
  between operations  14.2 us (5%)
  other arithmetic  6.48 us (2%)
    all_to_all x2, blocking collectives, exchange(): return lax.all_to_all(rows, axes, split_axis=0, concat_axis=0, tiled=True)  77.4 us
    all_to_all x5, waiting for transfers between devices, exchange(): return lax.all_to_all(rows, axes, split_axis=0, concat_axis=0, tiled=True)  56.5 us
    all_to_all x5, starting transfers between devices, exchange(): return lax.all_to_all(rows, axes, split_axis=0, concat_axis=0, tiled=True)  47 us
    pallas_call x1, Pallas kernels, local(): call_kernel(pick_kernel, ROWS_OUT, 'pick')  19.5 us
    pallas_call x1, Pallas kernels, local(): call_kernel(temporal_kernel, (MIXED_OUT, ROWS_OUT, GAIN_OUT), 'temporal')  12.6 us
    pallas_call x1, Pallas kernels, local(): call_kernel(spatial_forward_kernel, (ROWS_OUT, ROWS_OUT, QKV_OUT), 'spati...  9.27 us
    pallas_call x1, Pallas kernels, local(): call_kernel(spatial_backward_kernel, (ROWS_OUT, GAIN_OUT), 'spatial_backw...  9.09 us
  transfers between devices with their start and end apart: 9, of which 7 were waited for; matrix products, arithmetic and copies ran while one was open for 7% of the time, Pallas kernels for 5%

profile of v2, /device:TPU:1, one launch (start us, length us, event | category | flops | bytes accessed | tf_op | source)
XLA Modules:
  0.0 278.3 jit_solution(10260755670531976571)
XLA Ops:
  7.9 1.9 fusion.1
  9.9 0.9 dynamic-slice_bitcast_fusion.2
  10.8 0.8 dynamic-slice_bitcast_fusion
  11.9 1.2 broadcast_in_dim.34
  13.1 17.1 %all-to-all-start = ((bf16[64,2,2688]{2,1,0:T(2,128)(2,1)}), bf16[64,2,2688]{2,1,0:T(2,128)(2,1)S(1)}, u32[]{:S(2)}, u32[]{:S(2)}) async-start(bf16[64,2,2688]{2,1,0:T(2,128)(2,1)} %broadcast_in_dim.34), calls=%async_computation | async-start | bytes 1376256 | tf_op jit(solution)/shard_map/all_to_all | solution.py:262
  31.6 18.5 %all-to-all-done = bf16[64,2,2688]{2,1,0:T(2,128)(2,1)S(1)} async-done(((bf16[64,2,2688]{2,1,0:T(2,128)(2,1)}), bf16[64,2,2688]{2,1,0:T(2,128)(2,1)S(1)}, u32[]{:S(2)}, u32[]{:S(2)}) %all-to-all-start) | async-done | bytes 688160 | tf_op jit(solution)/shard_map/all_to_all | solution.py:262
  51.0 1.1 reshape.211
  52.5 1.0 maximum_maximum_fusion
  53.5 39.3 %all_to_all.35 = bf16[64,4,2560]{2,1,0:T(4,128)(2,1)S(1)} all-to-all(bf16[64,4,2560]{2,1,0:T(4,128)(2,1)S(1)} %pad_maximum_fusion), channel_id=1, replica_groups=mesh['rep'=8,'z'=8,'y'=8] {'z','y'}, dimensions={0} | all-to-all | bytes 2621440 | tf_op jit(solution)/shard_map/all_to_all | solution.py:262
  92.8 1.1 copy-done.4
  95.5 1.1 reshape.219
  96.9 1.0 maximum_maximum_fusion.1
  99.4 1.8 all-gather.11.cloned.1.call-done.full_hbm
  101.3 9.3 %spatial_forward.1 = (bf16[256,1152]{1,0:T(8,128)(2,1)S(1)}, bf16[256,1152]{1,0:T(8,128)(2,1)S(1)}, bf16[3,576,256]{2,1,0:T(8,128)(2,1)S(1)}) custom-call(s32[4]{0:T(128)S(1)} %multiply_add_fusion.1.starts, bf16[2176,1152]{1,0:T(8,128)(2,1)} %all-gather.9.cloned.1.call-done.everyone, f32[3,1152]{1,0:T(4,128)S(1)} %copy-done.1, ...), custom_call_target="tpu_custom_call" | custom-call | flops 6000000000 | bytes 8000000 | tf_op jit(solution)/shard_map/spatial_forward/pallas_call | solution.py:355
  110.6 1.0 reshape.216
  111.5 13.4 %all-to-all-start.2 = ((bf16[64,4,1152]{2,1,0:T(4,128)(2,1)}), bf16[64,4,1152]{2,1,0:T(4,128)(2,1)}, u32[]{:S(2)}, u32[]{:S(2)}) async-start(bf16[64,4,1152]{2,1,0:T(4,128)(2,1)} %reshape.216), calls=%async_computation.2 | async-start | bytes 1179648 | tf_op jit(solution)/shard_map/all_to_all | solution.py:262
  126.0 17.4 %all-to-all-done.2 = bf16[64,4,1152]{2,1,0:T(4,128)(2,1)} async-done(((bf16[64,4,1152]{2,1,0:T(4,128)(2,1)}), bf16[64,4,1152]{2,1,0:T(4,128)(2,1)}, u32[]{:S(2)}, u32[]{:S(2)}) %all-to-all-start.2) | async-done | bytes 589856 | tf_op jit(solution)/shard_map/all_to_all | solution.py:262
  143.5 1.5 reshape.217.v
  145.6 12.6 %temporal.1 = (bf16[256,576]{1,0:T(8,128)(2,1)S(1)}, bf16[256,1152]{1,0:T(8,128)(2,1)S(1)}, f32[3,1152]{1,0:T(4,128)S(1)}) custom-call(bf16[256,1152]{1,0:T(8,128)(2,1)S(1)} %reshape.215.g, bf16[256,1152]{1,0:T(8,128)(2,1)S(1)} %reshape.217.v, f32[3,1152]{1,0:T(4,128)S(1)} %copy-done, bf16[1152,2304]{1,0:T(8,128)(2,1)} %all-gather.13.cloned.1.call-done.full_hbm, ...), custom_call_target="tpu_custom_call" | custom-call | flops 6000000000 | bytes 8000000 | tf_op jit(solution)/shard_map/temporal/pallas_call | solution.py:368
  158.2 1.2 reshape.222
  159.4 38.1 %all_to_all.36 = bf16[64,4,1728]{2,1,0:T(4,128)(2,1)} all-to-all(bf16[64,4,1728]{2,1,0:T(4,128)(2,1)} %reshape.222), channel_id=1, replica_groups=mesh['rep'=8,'z'=8,'y'=8] {'z','y'}, dimensions={0} | all-to-all | bytes 1769472 | tf_op jit(solution)/shard_map/all_to_all | solution.py:262
  197.5 1.7 reshape.223
  199.3 9.1 %spatial_backward.1 = (bf16[256,1152]{1,0:T(8,128)(2,1)}, f32[3,1152]{1,0:T(4,128)S(1)}) custom-call(bf16[256,1152]{1,0:T(8,128)(2,1)S(1)} %slice.64.g, bf16[256,1152]{1,0:T(8,128)(2,1)S(1)} %copy-done.3, f32[3,1152]{1,0:T(4,128)S(1)} %copy-done.1, bf16[1152,2304]{1,0:T(8,128)(2,1)} %all-gather.11.cloned.1.call-done.full_hbm, s32[256,1]{1,0:T(8,128)S(1)} %select_n.32.lab_k, ...), custom_call_target="tpu_custom_call" | custom-call | flops 6000000000 | bytes 8000000 | tf_op jit(solution)/shard_map/spatial_backward/pallas_call | solution.py:376
  209.3 5.2 %all-to-all-start.4 = ((f32[8,8,864]{2,1,0:T(8,128)}), f32[8,8,864]{2,1,0:T(8,128)S(1)}, u32[]{:S(2)}, u32[]{:S(2)}) async-start(f32[8,8,864]{2,1,0:T(8,128)} %broadcast_in_dim.40), calls=%async_computation.4 | async-start | bytes 458752 | tf_op jit(solution)/shard_map/all_to_all | solution.py:262
  214.4 9.0 %all-to-all-done.4 = f32[8,8,864]{2,1,0:T(8,128)S(1)} async-done(((f32[8,8,864]{2,1,0:T(8,128)}), f32[8,8,864]{2,1,0:T(8,128)S(1)}, u32[]{:S(2)}, u32[]{:S(2)}) %all-to-all-start.4) | async-done | bytes 221216 | tf_op jit(solution)/shard_map/all_to_all | solution.py:262
  224.2 3.4 %all-to-all-start.5 = ((f32[8,8,864]{2,1,0:T(8,128)}), f32[8,8,864]{2,1,0:T(8,128)S(1)}, u32[]{:S(2)}, u32[]{:S(2)}) async-start(f32[8,8,864]{2,1,0:T(8,128)} %broadcast_in_dim.41), calls=%async_computation.5 | async-start | bytes 458752 | tf_op jit(solution)/shard_map/all_to_all | solution.py:262
  227.9 8.7 %all-to-all-done.5 = f32[8,8,864]{2,1,0:T(8,128)S(1)} async-done(((f32[8,8,864]{2,1,0:T(8,128)}), f32[8,8,864]{2,1,0:T(8,128)S(1)}, u32[]{:S(2)}, u32[]{:S(2)}) %all-to-all-start.5) | async-done | bytes 221216 | tf_op jit(solution)/shard_map/all_to_all | solution.py:262
  236.7 0.7 broadcast_in_dim.42
  237.4 7.9 %all-to-all-start.6 = ((f32[8,8,864]{2,1,0:T(8,128)}), f32[8,8,864]{2,1,0:T(8,128)S(1)}, u32[]{:S(2)}, u32[]{:S(2)}) async-start(f32[8,8,864]{2,1,0:T(8,128)} %broadcast_in_dim.42), calls=%async_computation.6 | async-start | bytes 458752 | tf_op jit(solution)/shard_map/all_to_all | solution.py:262
  245.3 3.4 %finish.1 = bf16[256,1152]{1,0:T(8,128)(2,1)} custom-call(bf16[256,1152]{1,0:T(8,128)(2,1)S(1)} %get-tuple-element.14.v, bf16[256,576]{1,0:T(8,128)(2,1)S(1)} %slice.63.mixed, bf16[1152,2304]{1,0:T(8,128)(2,1)} %all-gather.13.cloned.1.call-done.full_hbm), custom_call_target="tpu_custom_call" | custom-call | flops 6000000000 | bytes 8000000 | tf_op jit(solution)/shard_map/finish/pallas_call | solution.py:379
  248.7 2.8 %all-to-all-done.6 = f32[8,8,864]{2,1,0:T(8,128)S(1)} async-done(((f32[8,8,864]{2,1,0:T(8,128)}), f32[8,8,864]{2,1,0:T(8,128)S(1)}, u32[]{:S(2)}, u32[]{:S(2)}) %all-to-all-start.6) | async-done | bytes 221216 | tf_op jit(solution)/shard_map/all_to_all | solution.py:262
  252.2 19.5 %pick.1 = bf16[256,1152]{1,0:T(8,128)(2,1)} custom-call(s32[4]{0:T(128)S(1)} %multiply_add_fusion.starts, bf16[2048,1152]{1,0:T(8,128)(2,1)} %all-gather.15.cloned.1.call-done.everyone), custom_call_target="tpu_custom_call" | custom-call | flops 6000000000 | bytes 8000000 | tf_op jit(solution)/shard_map/pick/pallas_call | solution.py:381
  (93 shorter events, 11.4 us)
Async XLA Ops:
  7.2 91.1 %all-gather.9.cloned.1.call-start = ((), (), s32[]{:S(2)}) async-start(), calls=%async_computation.7 | async-start | bytes 5640192 | tf_op jit(solution)/shard_map/all_gather | solution.py:314
  9.8 20.8 %copy-start.5 = (bf16[4,1,64,1152]{3,2,1,0:T(8,128)(2,1)S(1)}, bf16[4,1,64,1152]{3,2,1,0:T(8,128)(2,1)}, u32[]{:S(2)}) copy-start(bf16[4,1,64,1152]{3,2,1,0:T(8,128)(2,1)} %param.21) | copy-start | bytes 1769476
  13.1 37.0 %all-to-all-start = ((bf16[64,2,2688]{2,1,0:T(2,128)(2,1)}), bf16[64,2,2688]{2,1,0:T(2,128)(2,1)S(1)}, u32[]{:S(2)}, u32[]{:S(2)}) async-start(bf16[64,2,2688]{2,1,0:T(2,128)(2,1)} %broadcast_in_dim.34), calls=%async_computation | async-start | bytes 1376256 | tf_op jit(solution)/shard_map/all_to_all | solution.py:262
  30.2 71.0 %all-gather.11.cloned.1.call-start = ((), (), s32[]{:S(2)}) async-start(), calls=%async_computation.8 | async-start | bytes 5971968 | tf_op jit(solution)/shard_map/all_gather | solution.py:285
  53.5 92.1 %all-gather.13.cloned.1.call-start = ((), (), s32[]{:S(2)}) async-start(), calls=%async_computation.9 | async-start | bytes 5971968 | tf_op jit(solution)/shard_map/all_gather | solution.py:285
  92.8 1.1 copy-start.4
  96.8 1.2 copy-start.7
  96.8 4.4 %copy-start.1 = (f32[3,1152]{1,0:T(4,128)S(1)}, f32[3,1152]{1,0:T(4,128)}, u32[]{:S(2)}) copy-start(f32[3,1152]{1,0:T(4,128)} %gains.5) | copy-start | bytes 41476
  110.5 15.3 %copy-start.2 = (bf16[256,1152]{1,0:T(8,128)(2,1)}, bf16[256,1152]{1,0:T(8,128)(2,1)S(1)}, u32[]{:S(2)}) copy-start(bf16[256,1152]{1,0:T(8,128)(2,1)S(1)} %get-tuple-element.18.v) | copy-start | bytes 1769476
  110.5 14.7 %copy-start.6 = (s32[4,4]{1,0:T(4,128)S(1)}, s32[4,4]{1,0:T(4,128)}, u32[]{:S(2)}) copy-start(s32[4,4]{1,0:T(4,128)} %param.14) | copy-start | bytes 196
  111.5 14.3 %slice-start = ((bf16[64,4,2560]{2,1,0:T(4,128)(2,1)}), bf16[64,4,1152]{2,1,0:T(4,128)(2,1)S(1)}, s32[]{:S(2)}) async-start(bf16[64,4,2560]{2,1,0:T(4,128)(2,1)} %copy-done.4), calls=%async_computation.11 | async-start | bytes 1179648 | tf_op jit(solution)/shard_map/slice | solution.py:336
  111.5 31.9 %all-to-all-start.2 = ((bf16[64,4,1152]{2,1,0:T(4,128)(2,1)}), bf16[64,4,1152]{2,1,0:T(4,128)(2,1)}, u32[]{:S(2)}, u32[]{:S(2)}) async-start(bf16[64,4,1152]{2,1,0:T(4,128)(2,1)} %reshape.216), calls=%async_computation.2 | async-start | bytes 1179648 | tf_op jit(solution)/shard_map/all_to_all | solution.py:262
  124.9 127.3 %all-gather.15.cloned.1.call-start = ((), (), s32[]{:S(2)}) async-start(), calls=%async_computation.10 | async-start | bytes 5308416 | tf_op jit(solution)/shard_map/all_gather | solution.py:380
  125.9 19.7 %copy-start = (f32[3,1152]{1,0:T(4,128)S(1)}, f32[3,1152]{1,0:T(4,128)}, u32[]{:S(2)}) copy-start(f32[3,1152]{1,0:T(4,128)} %gains.4) | copy-start | bytes 41476
  197.5 1.8 copy-start.3
  208.4 19.2 %copy-start.8 = (s32[4]{0:T(128)S(1)}, s32[4]{0:T(128)}, u32[]{:S(2)}) copy-start(s32[4]{0:T(128)} %param.12) | copy-start | bytes 52
  209.3 14.2 %all-to-all-start.4 = ((f32[8,8,864]{2,1,0:T(8,128)}), f32[8,8,864]{2,1,0:T(8,128)S(1)}, u32[]{:S(2)}, u32[]{:S(2)}) async-start(f32[8,8,864]{2,1,0:T(8,128)} %broadcast_in_dim.40), calls=%async_computation.4 | async-start | bytes 458752 | tf_op jit(solution)/shard_map/all_to_all | solution.py:262
  224.2 12.4 %all-to-all-start.5 = ((f32[8,8,864]{2,1,0:T(8,128)}), f32[8,8,864]{2,1,0:T(8,128)S(1)}, u32[]{:S(2)}, u32[]{:S(2)}) async-start(f32[8,8,864]{2,1,0:T(8,128)} %broadcast_in_dim.41), calls=%async_computation.5 | async-start | bytes 458752 | tf_op jit(solution)/shard_map/all_to_all | solution.py:262
  237.4 14.1 %all-to-all-start.6 = ((f32[8,8,864]{2,1,0:T(8,128)}), f32[8,8,864]{2,1,0:T(8,128)S(1)}, u32[]{:S(2)}, u32[]{:S(2)}) async-start(f32[8,8,864]{2,1,0:T(8,128)} %broadcast_in_dim.42), calls=%async_computation.6 | async-start | bytes 458752 | tf_op jit(solution)/shard_map/all_to_all | solution.py:262
Sparse Core Ops, SparseCore 0:
  10.1 46.7 all-gather.8
  59.0 42.1 all-gather.10
  103.4 42.1 all-gather.12
  208.6 35.5 all-gather.14

commit v3 on v2

--- a/solution.py
+++ b/solution.py
@@ -80,7 +80,8 @@
 
 def finish(v_ref, mixed, u_ref, out_ref):
     made = jnp.dot(mixed, u_ref[...].astype(jnp.bfloat16), preferred_element_type=jnp.float32)
-    out_ref[...] = (v_ref[...].astype(jnp.float32) + made).astype(jnp.bfloat16)
+    made = (v_ref[...].astype(jnp.float32) + made).astype(jnp.bfloat16)
+    out_ref[...] = made.reshape(out_ref.shape)
 
 
 def backward(
@@ -162,14 +163,15 @@
 
 
 def spatial_backward_kernel(
-    g, v, gains, full_hbm, lab_k, lab_q, qkv, grad, gain,
-    full, sems, u, q, k, x, o, dq, dk, dx,
+    both, v, gains, full_hbm, lab_k, lab_q, qkv, grad, gain,
+    full, sems, u, q, k, x, o, dq, dk, dx, g,
 ):
     copies = weight_copies(full_hbm, full, sems)
     for copy in copies[::-1]:
         copy.start()
     for which, ref in enumerate((q, k, x)):
         ref[...] = qkv[which].astype(jnp.float32)
+    g[...] = both[:, :, :1152].reshape(g.shape)
     copies[3].wait()
     copies[2].wait()
     load_u(full, u)
@@ -180,28 +182,34 @@
 
 
 def temporal_kernel(
-    g, v, gains, full_hbm, lab_k, lab_q, mixed, grad, gain,
-    full, sems, u, q, k, x, o, dq, dk, dx,
+    got, mid, gains, full_hbm, lab_k, lab_q, both, gain,
+    full, sems, u, q, k, x, o, dq, dk, dx, g, v, grad,
 ):
     copies = weight_copies(full_hbm, full, sems)
     for copy in copies:
         copy.start()
-    mixed[...] = forward(v, gains, full, copies, lab_k[...], lab_q[...], q, k, x, o)
+    v[...] = mid[...].reshape(v.shape)
+    g[...] = got[:, :, :1152].reshape(g.shape)
+    mixed = forward(v, gains, full, copies, lab_k[...], lab_q[...], q, k, x, o)
+    both[:, :, 1152:] = mixed.reshape(both.shape[0], both.shape[1], INNER)
     copies[3].wait()
     load_u(full, u)
     backward(
         g, v, gains, full, [], lab_k[...], lab_q[...], grad, gain, q, k, x, o, u, dq, dk, dx
     )
-
-
-def finish_kernel(v, mixed, full_hbm, out, full, sems, u):
+    both[:, :, :1152] = grad[...].reshape(both.shape[0], both.shape[1], 1152)
+
+
+def finish_kernel(mid, both, full_hbm, out, full, sems, u, v):
     copies = weight_copies(full_hbm, full, sems)[2:]
     for copy in copies:
         copy.start()
+    v[...] = mid[...].reshape(v.shape)
+    mixed = both[:, :, 1152:].reshape(v.shape[0], INNER)
     for copy in copies:
         copy.wait()
     load_u(full, u)
-    finish(v, mixed[...], u, out)
+    finish(v, mixed, u, out)
 
 
 def pick_kernel(starts, everyone, out, sems):
@@ -229,20 +237,23 @@
         pltpu.VMEM((1152, CUTS[-1]), jnp.bfloat16), four, pltpu.VMEM((INNER, 1152), jnp.float32)
     ]
     scratch += [pltpu.VMEM((INNER, rows), jnp.float32)] * 4
+    flat = pltpu.VMEM((rows, 1152), jnp.bfloat16)
+    backs = [pltpu.VMEM((640, rows), jnp.float32)] * 3
     if kernel is finish_kernel:
-        ins, scratch = [vmem, vmem, hbm], scratch[:3]
+        ins, scratch = [vmem, vmem, hbm], scratch[:3] + [flat]
     elif kernel is pick_kernel:
         ins, scratch = [smem, hbm], [four]
     elif kernel is spatial_forward_kernel:
         ins, scratch = [smem, hbm, vmem, hbm, vmem, vmem], scratch + [four]
+    elif kernel is temporal_kernel:
+        ins, scratch = [vmem] * 3 + [hbm] + [vmem] * 2, scratch + backs + [flat] * 3
     else:
-        ins = [vmem] * 3 + [hbm] + [vmem] * (2 if kernel is temporal_kernel else 3)
-        scratch = scratch + [pltpu.VMEM((640, rows), jnp.float32)] * 3
+        ins, scratch = [vmem] * 3 + [hbm] + [vmem] * 3, scratch + backs + [flat]
     return pl.pallas_call(
         kernel,
         out_shape=outs,
         in_specs=ins,
-        out_specs=hbm if kernel is pick_kernel else jax.tree.map(lambda _: vmem, outs),
+        out_specs=jax.tree.map(lambda _: vmem, outs),
         scratch_shapes=scratch,
         compiler_params=pltpu.CompilerParams(vmem_limit_bytes=50 * 1024 * 1024),
         cost_estimate=pl.CostEstimate(
@@ -253,7 +264,8 @@
 
 
 ROWS_OUT = jax.ShapeDtypeStruct((256, 1152), jnp.bfloat16)
-MIXED_OUT = jax.ShapeDtypeStruct((256, 576), jnp.bfloat16)
+MID_OUT = jax.ShapeDtypeStruct((64, 4, 1152), jnp.bfloat16)
+BOTH_OUT = jax.ShapeDtypeStruct((64, 4, 1728), jnp.bfloat16)
 GAIN_OUT = jax.ShapeDtypeStruct((3, 1152), jnp.float32)
 QKV_OUT = jax.ShapeDtypeStruct((3, 576, 256), jnp.bfloat16)
 
@@ -333,7 +345,6 @@
     full_t = gather_weights(
         mixed[:, :, width : width + piece // tokens].reshape(frames, -1), *sizes
     )
-    cot_tokens = mixed[:, :, :width].reshape(rows, width)
 
     dest_all = shared[:, rows, :bins_here].astype(jnp.int32)
     group_ids = jnp.arange(groups, dtype=jnp.int32)
@@ -353,9 +364,9 @@
     lab_k = jnp.where(key_ok, bin_ids[:, None], -1).reshape(rows, 1)
     lab_q = jnp.broadcast_to(bin_ids[:, None], (bins_here, slots)).reshape(1, rows)
     moved, mid, qkv = call_kernel(
-        spatial_forward_kernel, (ROWS_OUT, ROWS_OUT, QKV_OUT), "spatial_forward"
+        spatial_forward_kernel, (ROWS_OUT, MID_OUT, QKV_OUT), "spatial_forward"
     )(starts_here, shared.reshape(-1, width), gains_spatial, full_s, lab_k, lab_q)
-    mid_tokens = exchange(mid.reshape(frames, tokens, width), SEQ).reshape(rows, width)
+    mid_tokens = exchange(mid, SEQ)
 
     ends = jnp.cumsum(frame_counts, axis=1)
     video_id = jnp.sum(
@@ -365,23 +376,19 @@
     row_bin = place * tokens // slots
     video_row = jnp.sum((bin_ids == row_bin).astype(jnp.int32)[:, None] * video_id, axis=0)
     lab_t = video_row[:, None] * tokens + jnp.arange(tokens, dtype=jnp.int32)[None]
-    heads_tokens, mid_grad_tokens, grad_temporal = call_kernel(
-        temporal_kernel, (MIXED_OUT, ROWS_OUT, GAIN_OUT), "temporal"
-    )(cot_tokens, mid_tokens, gains_temporal, full_t, lab_t.reshape(rows, 1), lab_t.reshape(1, rows))
-
-    both = jnp.concatenate([mid_grad_tokens, heads_tokens], axis=1)
-    both = exchange(both.reshape(frames, tokens, width + inner), SEQ)
-    both = both.reshape(rows, width + inner)
-    mid_grad, heads_here = both[:, :width], both[:, width:]
+    both, grad_temporal = call_kernel(temporal_kernel, (BOTH_OUT, GAIN_OUT), "temporal")(
+        mixed, mid_tokens, gains_temporal, full_t, lab_t.reshape(rows, 1), lab_t.reshape(1, rows)
+    )
+    both = exchange(both, SEQ)
     moved_grad, grad_spatial = call_kernel(
         spatial_backward_kernel, (ROWS_OUT, GAIN_OUT), "spatial_backward"
-    )(mid_grad, moved, gains_spatial, full_s, lab_k, lab_q, qkv)
-    block_out = call_kernel(finish_kernel, ROWS_OUT, "finish")(mid, heads_here, full_t)
+    )(both, moved, gains_spatial, full_s, lab_k, lab_q, qkv)
+    block_out = call_kernel(finish_kernel, ROWS_OUT, "finish")(mid, both, full_t)
     returned = lax.all_gather(moved_grad, "rep", axis=0, tiled=False)
     latent_grad = call_kernel(pick_kernel, ROWS_OUT, "pick")(
         starts_back, returned.reshape(-1, width)
     )
-    sums = jnp.stack([grad_spatial, grad_temporal]).reshape(8, -1)
+    sums = jnp.stack([grad_spatial, grad_temporal]).reshape(-1, 128)
     for axis in ("y", "z", "rep"):
         sums = jnp.sum(spread(sums, axis), axis=0)
     gain_grads = sums.reshape((2,) + gains_spatial.shape)

time: 279 us -> 259 us (0.928)
  Pallas kernels: 53.9 us -> 38.9 us
  local copies, waits for them, and re-layouts: 19.9 us -> 14 us
    pallas_call x1, Pallas kernels: 19.5 us -> 2.52 us  [local(): call_kernel(pick_kernel, ROWS_OUT, 'pick')]
    reshape x5 -> x0, local copies, waits for them, and re-layouts: 5.43 us -> none  [the longest x1 1.71 us: local(): both = both.reshape(rows, width + inner)]
  transfers between devices with their start and end apart: 9 -> 9, of which waited for: 7 -> 7; matrix products, arithmetic and copies ran while one was open for 7% -> 7% of each run, Pallas kernels for 5% -> 6%
where the time goes in v3:
time: 259 us; the launch traced here: 258 us
  blocking collectives  77.2 us (30%)
  waiting for transfers between devices  60.4 us (23%)
  starting transfers between devices  47.1 us (18%)
  Pallas kernels  38.9 us (15%)
  between operations  14.2 us (5%)
  local copies, waits for them, and re-layouts  14 us (5%)
  other arithmetic  6.39 us (2%)
    all_to_all x2, blocking collectives, exchange(): return lax.all_to_all(rows, axes, split_axis=0, concat_axis=0, tiled=True)  77.2 us
    all_to_all x5, waiting for transfers between devices, exchange(): return lax.all_to_all(rows, axes, split_axis=0, concat_axis=0, tiled=True)  55.8 us
    all_to_all x5, starting transfers between devices, exchange(): return lax.all_to_all(rows, axes, split_axis=0, concat_axis=0, tiled=True)  46.7 us
    pallas_call x1, Pallas kernels, local(): call_kernel(temporal_kernel, (BOTH_OUT, GAIN_OUT), 'temporal')  12.7 us
    pallas_call x1, Pallas kernels, local(): call_kernel(spatial_forward_kernel, (ROWS_OUT, MID_OUT, QKV_OUT), 'spatia...  10.1 us
    pallas_call x1, Pallas kernels, local(): call_kernel(spatial_backward_kernel, (ROWS_OUT, GAIN_OUT), 'spatial_backw...  9.11 us
  transfers between devices with their start and end apart: 9, of which 7 were waited for; matrix products, arithmetic and copies ran while one was open for 7% of the time, Pallas kernels for 6%

profile of v3, /device:TPU:1, one launch (start us, length us, event | category | flops | bytes accessed | tf_op | source)
XLA Modules:
  0.0 258.1 jit_solution(865273170099188361)
XLA Ops:
  7.9 2.0 fusion.1
  9.9 0.9 dynamic-slice_bitcast_fusion.2
  10.8 0.8 dynamic-slice_bitcast_fusion
  11.9 1.2 broadcast_in_dim.34
  13.1 17.1 %all-to-all-start = ((bf16[64,2,2688]{2,1,0:T(2,128)(2,1)}), bf16[64,2,2688]{2,1,0:T(2,128)(2,1)S(1)}, u32[]{:S(2)}, u32[]{:S(2)}) async-start(bf16[64,2,2688]{2,1,0:T(2,128)(2,1)} %broadcast_in_dim.34), calls=%async_computation | async-start | bytes 1376256 | tf_op jit(solution)/shard_map/all_to_all | solution.py:274
  31.6 18.5 %all-to-all-done = bf16[64,2,2688]{2,1,0:T(2,128)(2,1)S(1)} async-done(((bf16[64,2,2688]{2,1,0:T(2,128)(2,1)}), bf16[64,2,2688]{2,1,0:T(2,128)(2,1)S(1)}, u32[]{:S(2)}, u32[]{:S(2)}) %all-to-all-start) | async-done | bytes 688160 | tf_op jit(solution)/shard_map/all_to_all | solution.py:274
  51.0 1.1 reshape.196
  52.5 1.0 maximum_maximum_fusion
  53.5 39.3 %all_to_all.35.got = bf16[64,4,2560]{2,1,0:T(4,128)(2,1)S(1)} all-to-all(bf16[64,4,2560]{2,1,0:T(4,128)(2,1)S(1)} %pad_maximum_fusion), channel_id=1, replica_groups=mesh['rep'=8,'z'=8,'y'=8] {'z','y'}, dimensions={0} | all-to-all | bytes 2621440 | tf_op jit(solution)/shard_map/all_to_all | solution.py:274
  94.4 1.1 reshape.201
  95.8 1.0 maximum_maximum_fusion.1
  97.2 0.7 slice.40
  98.3 2.9 %all-gather.11.cloned.1.call-done.full_hbm = bf16[1152,2304]{1,0:T(8,128)(2,1)} async-done(((bf16[144,2304]{1,0:T(8,128)(2,1)}), bf16[1152,2304]{1,0:T(8,128)(2,1)}) %all-gather.11.cloned.1.call-update) | async-done | bytes 5308432 | tf_op jit(solution)/shard_map/all_gather | solution.py:297
  101.3 10.1 %spatial_forward.1 = (bf16[256,1152]{1,0:T(8,128)(2,1)S(1)}, bf16[64,4,1152]{2,1,0:T(4,128)(2,1)}, bf16[3,576,256]{2,1,0:T(8,128)(2,1)S(1)}) custom-call(s32[4]{0:T(128)S(1)} %multiply_add_fusion.1.starts, bf16[2176,1152]{1,0:T(8,128)(2,1)} %all-gather.9.cloned.1.call-done.everyone, f32[3,1152]{1,0:T(4,128)S(1)} %copy-done.1, ...), custom_call_target="tpu_custom_call" | custom-call | flops 6000000000 | bytes 8000000 | tf_op jit(solution)/shard_map/spatial_forward/pallas_call | solution.py:366
  111.4 0.8 copy-done.2
  112.2 13.1 %all-to-all-start.2 = ((bf16[64,4,1152]{2,1,0:T(4,128)(2,1)}), bf16[64,4,1152]{2,1,0:T(4,128)(2,1)S(1)}, u32[]{:S(2)}, u32[]{:S(2)}) async-start(bf16[64,4,1152]{2,1,0:T(4,128)(2,1)} %get-tuple-element.13.mid), calls=%async_computation.2 | async-start | bytes 1179648 | tf_op jit(solution)/shard_map/all_to_all | solution.py:274
  126.2 17.8 %all-to-all-done.2.mid = bf16[64,4,1152]{2,1,0:T(4,128)(2,1)S(1)} async-done(((bf16[64,4,1152]{2,1,0:T(4,128)(2,1)}), bf16[64,4,1152]{2,1,0:T(4,128)(2,1)S(1)}, u32[]{:S(2)}, u32[]{:S(2)}) %all-to-all-start.2) | async-done | bytes 589856 | tf_op jit(solution)/shard_map/all_to_all | solution.py:274
  144.0 1.6 all-gather.13.cloned.1.call-done.full_hbm
  145.6 12.7 %temporal.1 = (bf16[64,4,1728]{2,1,0:T(4,128)(2,1)S(1)}, f32[3,1152]{1,0:T(4,128)S(1)}) custom-call(bf16[64,4,2560]{2,1,0:T(4,128)(2,1)S(1)} %all_to_all.35.got, bf16[64,4,1152]{2,1,0:T(4,128)(2,1)S(1)} %all-to-all-done.2.mid, f32[3,1152]{1,0:T(4,128)S(1)} %copy-done, bf16[1152,2304]{1,0:T(8,128)(2,1)} %all-gather.13.cloned.1.call-done.full_hbm, ...), custom_call_target="tpu_custom_call" | custom-call | flops 6000000000 | bytes 8000000 | tf_op jit(solution)/shard_map/temporal/pallas_call | solution.py:379
  158.3 38.0 %all_to_all.36.both = bf16[64,4,1728]{2,1,0:T(4,128)(2,1)S(1)} all-to-all(bf16[64,4,1728]{2,1,0:T(4,128)(2,1)S(1)} %get-tuple-element.15), channel_id=1, replica_groups=mesh['rep'=8,'z'=8,'y'=8] {'z','y'}, dimensions={0} | all-to-all | bytes 1769472 | tf_op jit(solution)/shard_map/all_to_all | solution.py:274
  196.3 9.1 %spatial_backward.1 = (bf16[256,1152]{1,0:T(8,128)(2,1)}, f32[3,1152]{1,0:T(4,128)S(1)}) custom-call(bf16[64,4,1728]{2,1,0:T(4,128)(2,1)S(1)} %all_to_all.36.both, bf16[256,1152]{1,0:T(8,128)(2,1)S(1)} %copy-done.3, f32[3,1152]{1,0:T(4,128)S(1)} %copy-done.1, bf16[1152,2304]{1,0:T(8,128)(2,1)} %all-gather.11.cloned.1.call-done.full_hbm, ...), custom_call_target="tpu_custom_call" | custom-call | flops 6000000000 | bytes 8000000 | tf_op jit(solution)/shard_map/spatial_backward/pallas_call | solution.py:383
  205.5 0.7 broadcast_in_dim.40
  206.2 5.2 %all-to-all-start.4 = ((f32[8,54,128]{2,1,0:T(8,128)}), f32[8,54,128]{2,1,0:T(8,128)S(1)}, u32[]{:S(2)}, u32[]{:S(2)}) async-start(f32[8,54,128]{2,1,0:T(8,128)} %broadcast_in_dim.40), calls=%async_computation.4 | async-start | bytes 458752 | tf_op jit(solution)/shard_map/all_to_all | solution.py:274
  211.4 9.0 %all-to-all-done.4 = f32[8,54,128]{2,1,0:T(8,128)S(1)} async-done(((f32[8,54,128]{2,1,0:T(8,128)}), f32[8,54,128]{2,1,0:T(8,128)S(1)}, u32[]{:S(2)}, u32[]{:S(2)}) %all-to-all-start.4) | async-done | bytes 221216 | tf_op jit(solution)/shard_map/all_to_all | solution.py:274
  220.4 0.7 broadcast_in_dim.41
  221.1 3.4 %all-to-all-start.5 = ((f32[8,54,128]{2,1,0:T(8,128)}), f32[8,54,128]{2,1,0:T(8,128)S(1)}, u32[]{:S(2)}, u32[]{:S(2)}) async-start(f32[8,54,128]{2,1,0:T(8,128)} %broadcast_in_dim.41), calls=%async_computation.5 | async-start | bytes 458752 | tf_op jit(solution)/shard_map/all_to_all | solution.py:274
  224.8 8.8 %all-to-all-done.5 = f32[8,54,128]{2,1,0:T(8,128)S(1)} async-done(((f32[8,54,128]{2,1,0:T(8,128)}), f32[8,54,128]{2,1,0:T(8,128)S(1)}, u32[]{:S(2)}, u32[]{:S(2)}) %all-to-all-start.5) | async-done | bytes 221216 | tf_op jit(solution)/shard_map/all_to_all | solution.py:274
  233.6 0.7 broadcast_in_dim.42
  234.3 7.9 %all-to-all-start.6 = ((f32[8,54,128]{2,1,0:T(8,128)}), f32[8,54,128]{2,1,0:T(8,128)S(1)}, u32[]{:S(2)}, u32[]{:S(2)}) async-start(f32[8,54,128]{2,1,0:T(8,128)} %broadcast_in_dim.42), calls=%async_computation.6 | async-start | bytes 458752 | tf_op jit(solution)/shard_map/all_to_all | solution.py:274
  242.2 4.5 %finish.1 = bf16[256,1152]{1,0:T(8,128)(2,1)} custom-call(bf16[64,4,1152]{2,1,0:T(4,128)(2,1)} %get-tuple-element.13.mid, bf16[64,4,1728]{2,1,0:T(4,128)(2,1)S(1)} %all_to_all.36.both, bf16[1152,2304]{1,0:T(8,128)(2,1)} %all-gather.13.cloned.1.call-done.full_hbm), custom_call_target="tpu_custom_call" | custom-call | flops 6000000000 | bytes 8000000 | tf_op jit(solution)/shard_map/finish/pallas_call | solution.py:386
  246.6 1.7 all-to-all-done.6
  249.0 2.5 pick.1
  (81 shorter events, 8.2 us)
Async XLA Ops:
  7.2 90.0 %all-gather.9.cloned.1.call-start = ((), (), s32[]{:S(2)}) async-start(), calls=%async_computation.7 | async-start | bytes 5640192 | tf_op jit(solution)/shard_map/all_gather | solution.py:326
  9.8 20.8 %copy-start.4 = (bf16[4,1,64,1152]{3,2,1,0:T(8,128)(2,1)S(1)}, bf16[4,1,64,1152]{3,2,1,0:T(8,128)(2,1)}, u32[]{:S(2)}) copy-start(bf16[4,1,64,1152]{3,2,1,0:T(8,128)(2,1)} %param.21) | copy-start | bytes 1769476
  13.1 37.0 %all-to-all-start = ((bf16[64,2,2688]{2,1,0:T(2,128)(2,1)}), bf16[64,2,2688]{2,1,0:T(2,128)(2,1)S(1)}, u32[]{:S(2)}, u32[]{:S(2)}) async-start(bf16[64,2,2688]{2,1,0:T(2,128)(2,1)} %broadcast_in_dim.34), calls=%async_computation | async-start | bytes 1376256 | tf_op jit(solution)/shard_map/all_to_all | solution.py:274
  30.2 71.0 %all-gather.11.cloned.1.call-start = ((), (), s32[]{:S(2)}) async-start(), calls=%async_computation.8 | async-start | bytes 5971968 | tf_op jit(solution)/shard_map/all_gather | solution.py:297
  53.5 92.1 %all-gather.13.cloned.1.call-start = ((), (), s32[]{:S(2)}) async-start(), calls=%async_computation.9 | async-start | bytes 5971968 | tf_op jit(solution)/shard_map/all_gather | solution.py:297
  95.7 1.2 copy-start.6
  95.7 5.5 %copy-start.1 = (f32[3,1152]{1,0:T(4,128)S(1)}, f32[3,1152]{1,0:T(4,128)}, u32[]{:S(2)}) copy-start(f32[3,1152]{1,0:T(4,128)} %gains.5) | copy-start | bytes 41476
  98.3 27.3 %copy-start.5 = (s32[4,4]{1,0:T(4,128)S(1)}, s32[4,4]{1,0:T(4,128)}, u32[]{:S(2)}) copy-start(s32[4,4]{1,0:T(4,128)} %param.14) | copy-start | bytes 196
  111.3 0.8 copy-start.2
  112.2 33.4 %copy-start = (f32[3,1152]{1,0:T(4,128)S(1)}, f32[3,1152]{1,0:T(4,128)}, u32[]{:S(2)}) copy-start(f32[3,1152]{1,0:T(4,128)} %gains.4) | copy-start | bytes 41476
  112.2 31.9 %all-to-all-start.2 = ((bf16[64,4,1152]{2,1,0:T(4,128)(2,1)}), bf16[64,4,1152]{2,1,0:T(4,128)(2,1)S(1)}, u32[]{:S(2)}, u32[]{:S(2)}) async-start(bf16[64,4,1152]{2,1,0:T(4,128)(2,1)} %get-tuple-element.13.mid), calls=%async_computation.2 | async-start | bytes 1179648 | tf_op jit(solution)/shard_map/all_to_all | solution.py:274
  125.3 123.7 %all-gather.15.cloned.1.call-start = ((), (), s32[]{:S(2)}) async-start(), calls=%async_computation.10 | async-start | bytes 5308416 | tf_op jit(solution)/shard_map/all_gather | solution.py:387
  158.3 38.0 %copy-start.3 = (bf16[256,1152]{1,0:T(8,128)(2,1)S(1)}, bf16[256,1152]{1,0:T(8,128)(2,1)}, u32[]{:S(2)}) copy-start(bf16[256,1152]{1,0:T(8,128)(2,1)} %copy-done.2) | copy-start | bytes 1769476
  205.4 19.1 %copy-start.7 = (s32[4]{0:T(128)S(1)}, s32[4]{0:T(128)}, u32[]{:S(2)}) copy-start(s32[4]{0:T(128)} %param.12) | copy-start | bytes 52
  206.2 14.2 %all-to-all-start.4 = ((f32[8,54,128]{2,1,0:T(8,128)}), f32[8,54,128]{2,1,0:T(8,128)S(1)}, u32[]{:S(2)}, u32[]{:S(2)}) async-start(f32[8,54,128]{2,1,0:T(8,128)} %broadcast_in_dim.40), calls=%async_computation.4 | async-start | bytes 458752 | tf_op jit(solution)/shard_map/all_to_all | solution.py:274
  221.1 12.4 %all-to-all-start.5 = ((f32[8,54,128]{2,1,0:T(8,128)}), f32[8,54,128]{2,1,0:T(8,128)S(1)}, u32[]{:S(2)}, u32[]{:S(2)}) async-start(f32[8,54,128]{2,1,0:T(8,128)} %broadcast_in_dim.41), calls=%async_computation.5 | async-start | bytes 458752 | tf_op jit(solution)/shard_map/all_to_all | solution.py:274
  234.3 14.1 %all-to-all-start.6 = ((f32[8,54,128]{2,1,0:T(8,128)}), f32[8,54,128]{2,1,0:T(8,128)S(1)}, u32[]{:S(2)}, u32[]{:S(2)}) async-start(f32[8,54,128]{2,1,0:T(8,128)} %broadcast_in_dim.42), calls=%async_computation.6 | async-start | bytes 458752 | tf_op jit(solution)/shard_map/all_to_all | solution.py:274
Sparse Core Ops, SparseCore 0:
  10.1 46.7 all-gather.8
  59.0 42.1 all-gather.10
  103.4 42.1 all-gather.12
  205.6 35.5 all-gather.14

commit v4 on v3

--- a/solution.py
+++ b/solution.py
@@ -16,17 +16,51 @@
 U_FROM = 1664
 
 
-def scores_of(q_ref, k_ref, head, allowed):
-    rows = slice(HD * head, HD * head + HD)
-    query = q_ref[rows, :].astype(jnp.bfloat16)
-    keys = k_ref[rows, :].astype(jnp.bfloat16)
-    raw = lax.dot_general(
-        keys, query, (((0,), (0,)), ((), ())), preferred_element_type=jnp.float32
-    )
-    raw = jnp.where(allowed, raw * (1.0 / math.sqrt(HD)), -1000000000.0)
-    expo = jnp.exp(raw - jnp.max(raw, axis=0, keepdims=True))
-    weights = expo * (1.0 / jnp.sum(expo, axis=0, keepdims=True))
-    return query, keys, weights
+OVER_ROWS = (((0,), (0,)), ((), ()))
+OVER_LANES = (((1,), (1,)), ((), ()))
+TO_POWER = math.log2(math.e) / math.sqrt(HD)
+
+
+def softmax_of(raw, allowed):
+    raw = jnp.where(allowed, raw * TO_POWER, -1000000000.0)
+    expo = jnp.exp2(raw - jnp.max(raw, axis=0, keepdims=True))
+    return expo * (1.0 / jnp.sum(expo, axis=0, keepdims=True))
+
+
+def frame_blocks(left, right):
+    lane = lax.broadcasted_iota(jnp.int32, (64, 128), 1)
+    halves = []
+    for half in range(2):
+        lanes = slice(128 * half, 128 * half + 128)
+        made = lax.dot_general(
+            left[:, lanes], right[:, lanes], OVER_ROWS, preferred_element_type=jnp.float32
+        )
+        halves.append(jnp.where(lane < 64, made[:64], made[64:]))
+    return jnp.concatenate(halves, axis=1)
+
+
+def spread_blocks(blocks):
+    lane = lax.broadcasted_iota(jnp.int32, (64, 128), 1)
+    squares = []
+    for half in range(2):
+        block = blocks[:, 128 * half : 128 * half + 128]
+        pair = [jnp.where(lane < 64, block, 0.0), jnp.where(lane < 64, 0.0, block)]
+        squares.append(jnp.concatenate(pair, axis=0).astype(jnp.bfloat16))
+    return squares
+
+
+def times_squares(left, squares, dims):
+    made = [
+        lax.dot_general(
+            left[:, 128 * half : 128 * half + 128], squares[half], dims,
+            preferred_element_type=jnp.float32,
+        )
+        for half in range(2)
+    ]
+    return jnp.concatenate(made, axis=1)
+
+
+FORWARD_DIMS = (((1,), (0,)), ((), ()))
 
 
 def normed_of(v_ref):
@@ -55,26 +89,33 @@
         u_ref[rows, 640:] = right[:, 128:]
 
 
-def forward(v_ref, gains_ref, full_ref, copies, key_label, query_label, q_ref, k_ref, x_ref, o_ref):
+def forward(v_ref, gains_ref, full_ref, copies, allowed, q_ref, k_ref, x_ref, o_ref, w_ref):
     normed, scale = normed_of(v_ref)
 
     def project(which, first, past):
         copies[which].wait()
         scaled = (normed * gains_ref[which : which + 1, :]).astype(jnp.bfloat16)
         made = jnp.dot(scaled, full_ref[:, first:past], preferred_element_type=jnp.float32)
-        return jnp.transpose(made)
+        return jnp.transpose(made.astype(jnp.bfloat16)).astype(jnp.float32)
 
     q_ref[...] = project(0, 0, 640)[:INNER]
     k_ref[...] = project(1, 512, 1152)[64:]
     x_ref[...] = project(2, 1152, 1792)[:INNER]
-    allowed = key_label == query_label
     for head in range(HEADS):
         rows = slice(HD * head, HD * head + HD)
-        _, _, weights = scores_of(q_ref, k_ref, head, allowed)
+        query = q_ref[rows, :].astype(jnp.bfloat16)
+        keys = k_ref[rows, :].astype(jnp.bfloat16)
         vals = x_ref[rows, :].astype(jnp.bfloat16)
-        o_ref[rows, :] = jnp.dot(
-            vals, weights.astype(jnp.bfloat16), preferred_element_type=jnp.float32
-        )
+        if w_ref is None:
+            weights = softmax_of(frame_blocks(keys, query), allowed)
+            o_ref[rows, :] = times_squares(vals, spread_blocks(weights), FORWARD_DIMS)
+        else:
+            raw = lax.dot_general(keys, query, OVER_ROWS, preferred_element_type=jnp.float32)
+            weights = softmax_of(raw, allowed)
+            w_ref[head] = weights
+            o_ref[rows, :] = jnp.dot(
+                vals, weights.astype(jnp.bfloat16), preferred_element_type=jnp.float32
+            )
     return jnp.transpose(o_ref[...]).astype(jnp.bfloat16)
 
 
@@ -85,8 +126,8 @@
 
 
 def backward(
-    g_ref, v_ref, gains_ref, full_ref, copies, key_label, query_label, grad_ref, gain_ref,
-    q_ref, k_ref, x_ref, o_ref, u_ref, dq_ref, dk_ref, dx_ref,
+    g_ref, v_ref, gains_ref, full_ref, copies, allowed, grad_ref, gain_ref,
+    q_ref, k_ref, x_ref, o_ref, u_ref, dq_ref, dk_ref, dx_ref, w_ref,
 ):
     grad = g_ref[...]
     o_ref[...] = lax.dot_general(
@@ -99,27 +140,36 @@
     dq_ref[INNER:, :] = zeros
     dk_ref[: 640 - INNER, :] = zeros
     dx_ref[INNER:, :] = zeros
-    allowed = key_label == query_label
-    over_lanes = (((1,), (1,)), ((), ()))
     for head in range(HEADS):
         low = HD * head
         rows = slice(low, low + HD)
-        query, keys, weights = scores_of(q_ref, k_ref, head, allowed)
+        query = q_ref[rows, :].astype(jnp.bfloat16)
+        keys = k_ref[rows, :].astype(jnp.bfloat16)
         vals = x_ref[rows, :].astype(jnp.bfloat16)
         d_out = o_ref[rows, :].astype(jnp.bfloat16)
-        d_weights = lax.dot_general(
-            vals, d_out, (((0,), (0,)), ((), ())), preferred_element_type=jnp.float32
-        )
+        if w_ref is None:
+            weights = softmax_of(frame_blocks(keys, query), allowed)
+            d_weights = frame_blocks(vals, d_out)
+        else:
+            weights = w_ref[head]
+            d_weights = lax.dot_general(
+                vals, d_out, OVER_ROWS, preferred_element_type=jnp.float32
+            )
         along = jnp.sum(d_weights * weights, axis=0, keepdims=True)
-        d_scores = weights * (d_weights - along) * (1.0 / math.sqrt(HD))
-        d_scores = d_scores.astype(jnp.bfloat16)
-        dq_ref[rows, :] = jnp.dot(keys, d_scores, preferred_element_type=jnp.float32)
-        dk_ref[64 + low : 64 + low + HD, :] = lax.dot_general(
-            query, d_scores, over_lanes, preferred_element_type=jnp.float32
-        )
-        dx_ref[rows, :] = lax.dot_general(
-            d_out, weights.astype(jnp.bfloat16), over_lanes, preferred_element_type=jnp.float32
-        )
+        d_scores = weights * ((d_weights - along) * (1.0 / math.sqrt(HD)))
+        if w_ref is None:
+            d_scores, weights = spread_blocks(d_scores), spread_blocks(weights)
+            dq = times_squares(keys, d_scores, FORWARD_DIMS)
+            dk = times_squares(query, d_scores, OVER_LANES)
+            dx = times_squares(d_out, weights, OVER_LANES)
+        else:
+            d_scores, weights = d_scores.astype(jnp.bfloat16), weights.astype(jnp.bfloat16)
+            dq = jnp.dot(keys, d_scores, preferred_element_type=jnp.float32)
+            dk = lax.dot_general(query, d_scores, OVER_LANES, preferred_element_type=jnp.float32)
+            dx = lax.dot_general(d_out, weights, OVER_LANES, preferred_element_type=jnp.float32)
+        dq_ref[rows, :] = dq
+        dk_ref[64 + low : 64 + low + HD, :] = dk
+        dx_ref[rows, :] = dx
     normed, scale = normed_of(v_ref)
     for copy in copies:
         copy.wait()
@@ -127,7 +177,7 @@
     for which, (ref, first) in enumerate(((dq_ref, 0), (dk_ref, 512), (dx_ref, 1152))):
         made = jnp.transpose(ref[...]).astype(jnp.bfloat16)
         back = lax.dot_general(
-            made, full_ref[:, first : first + 640], over_lanes, preferred_element_type=jnp.float32
+            made, full_ref[:, first : first + 640], OVER_LANES, preferred_element_type=jnp.float32
         )
         gain_ref[which : which + 1, :] = jnp.sum(back * normed, axis=0, keepdims=True)
         term = back * gains_ref[which : which + 1, :]
@@ -137,8 +187,12 @@
     grad_ref[...] = result.astype(jnp.bfloat16)
 
 
+def valid_keys(counts):
+    return lax.broadcasted_iota(jnp.int32, (64, 256), 0) < counts[...]
+
+
 def spatial_forward_kernel(
-    starts, everyone, gains, full_hbm, lab_k, lab_q, moved, mid, qkv,
+    starts, everyone, gains, full_hbm, counts, moved, mid, qkv,
     full, sems, u, q, k, x, o, pick_sems,
 ):
     copies = weight_copies(full_hbm, full, sems)
@@ -150,11 +204,13 @@
         )
         for i in range(4)
     ]
-    for copy in picks + copies:
+    for copy in picks + copies[:1]:
         copy.start()
     for copy in picks:
         copy.wait()
-    mixed = forward(moved, gains, full, copies, lab_k[...], lab_q[...], q, k, x, o)
+    for copy in copies[1:]:
+        copy.start()
+    mixed = forward(moved, gains, full, copies, valid_keys(counts), q, k, x, o, None)
     copies[3].wait()
     load_u(full, u)
     finish(moved, mixed, u, mid)
@@ -163,7 +219,7 @@
 
 
 def spatial_backward_kernel(
-    both, v, gains, full_hbm, lab_k, lab_q, qkv, grad, gain,
+    both, v, gains, full_hbm, counts, qkv, grad, gain,
     full, sems, u, q, k, x, o, dq, dk, dx, g,
 ):
     copies = weight_copies(full_hbm, full, sems)
@@ -176,26 +232,27 @@
     copies[2].wait()
     load_u(full, u)
     backward(
-        g, v, gains, full, copies[:2], lab_k[...], lab_q[...], grad, gain,
-        q, k, x, o, u, dq, dk, dx,
+        g, v, gains, full, copies[:2], valid_keys(counts), grad, gain,
+        q, k, x, o, u, dq, dk, dx, None,
     )
 
 
 def temporal_kernel(
     got, mid, gains, full_hbm, lab_k, lab_q, both, gain,
-    full, sems, u, q, k, x, o, dq, dk, dx, g, v, grad,
+    full, sems, u, q, k, x, o, dq, dk, dx, g, v, grad, w,
 ):
     copies = weight_copies(full_hbm, full, sems)
     for copy in copies:
         copy.start()
     v[...] = mid[...].reshape(v.shape)
     g[...] = got[:, :, :1152].reshape(g.shape)
-    mixed = forward(v, gains, full, copies, lab_k[...], lab_q[...], q, k, x, o)
+    allowed = lab_k[...] == lab_q[...]
+    mixed = forward(v, gains, full, copies, allowed, q, k, x, o, w)
     both[:, :, 1152:] = mixed.reshape(both.shape[0], both.shape[1], INNER)
     copies[3].wait()
     load_u(full, u)
     backward(
-        g, v, gains, full, [], lab_k[...], lab_q[...], grad, gain, q, k, x, o, u, dq, dk, dx
+        g, v, gains, full, [], allowed, grad, gain, q, k, x, o, u, dq, dk, dx, w
     )
     both[:, :, :1152] = grad[...].reshape(both.shape[0], both.shape[1], 1152)
 
@@ -244,11 +301,12 @@
     elif kernel is pick_kernel:
         ins, scratch = [smem, hbm], [four]
     elif kernel is spatial_forward_kernel:
-        ins, scratch = [smem, hbm, vmem, hbm, vmem, vmem], scratch + [four]
+        ins, scratch = [smem, hbm, vmem, hbm, vmem], scratch + [four]
     elif kernel is temporal_kernel:
         ins, scratch = [vmem] * 3 + [hbm] + [vmem] * 2, scratch + backs + [flat] * 3
+        scratch = scratch + [pltpu.VMEM((HEADS, rows, rows), jnp.float32)]
     else:
-        ins, scratch = [vmem] * 3 + [hbm] + [vmem] * 3, scratch + backs + [flat]
+        ins, scratch = [vmem] * 3 + [hbm] + [vmem] * 2, scratch + backs + [flat]
     return pl.pallas_call(
         kernel,
         out_shape=outs,
@@ -360,12 +418,10 @@
 
     starts_here = from_group * shared.shape[1] + from_bin * slots
     starts_back = destination * rows + rank * slots
-    key_ok = jnp.arange(slots, dtype=jnp.int32)[None, :] < token_counts
-    lab_k = jnp.where(key_ok, bin_ids[:, None], -1).reshape(rows, 1)
-    lab_q = jnp.broadcast_to(bin_ids[:, None], (bins_here, slots)).reshape(1, rows)
+    counts = jnp.broadcast_to(token_counts, (bins_here, slots)).reshape(1, rows)
     moved, mid, qkv = call_kernel(
         spatial_forward_kernel, (ROWS_OUT, MID_OUT, QKV_OUT), "spatial_forward"
-    )(starts_here, shared.reshape(-1, width), gains_spatial, full_s, lab_k, lab_q)
+    )(starts_here, shared.reshape(-1, width), gains_spatial, full_s, counts)
     mid_tokens = exchange(mid, SEQ)
 
     ends = jnp.cumsum(frame_counts, axis=1)
@@ -382,7 +438,7 @@
     both = exchange(both, SEQ)
     moved_grad, grad_spatial = call_kernel(
         spatial_backward_kernel, (ROWS_OUT, GAIN_OUT), "spatial_backward"
-    )(both, moved, gains_spatial, full_s, lab_k, lab_q, qkv)
+    )(both, moved, gains_spatial, full_s, counts, qkv)
     block_out = call_kernel(finish_kernel, ROWS_OUT, "finish")(mid, both, full_t)
     returned = lax.all_gather(moved_grad, "rep", axis=0, tiled=False)
     latent_grad = call_kernel(pick_kernel, ROWS_OUT, "pick")(
@@ -390,7 +446,8 @@
     )
     sums = jnp.stack([grad_spatial, grad_temporal]).reshape(-1, 128)
     for axis in ("y", "z", "rep"):
-        sums = jnp.sum(spread(sums, axis), axis=0)
+        sent = sums.astype(jnp.bfloat16)
+        sums = jnp.sum(spread(sent, axis).astype(jnp.float32), axis=0)
     gain_grads = sums.reshape((2,) + gains_spatial.shape)
     return (block_out.reshape(latents.shape), latent_grad.reshape(latents.shape), gain_grads)
 

time: 259 us -> 254 us (0.981)
  Pallas kernels: 38.9 us -> 35.3 us
    all_to_all x5, waiting for transfers between devices: 55.8 us -> 52 us  [exchange(): return lax.all_to_all(rows, axes, split_axis=0, concat_axis=0, tiled=True)]
  transfers between devices with their start and end apart: 9 -> 9, of which waited for: 7 -> 7; matrix products, arithmetic and copies ran while one was open for 7% -> 7% of each run, Pallas kernels for 6% -> 5%
where the time goes in v4:
time: 254 us; the launch traced here: 253 us
  blocking collectives  77.2 us (30%)
  waiting for transfers between devices  58.9 us (23%)
  starting transfers between devices  47.2 us (19%)
  Pallas kernels  35.3 us (14%)
  between operations  14.2 us (6%)
  local copies, waits for them, and re-layouts  13.8 us (5%)
  other arithmetic  6.4 us (3%)
    all_to_all x2, blocking collectives, exchange(): return lax.all_to_all(rows, axes, split_axis=0, concat_axis=0, tiled=True)  77.2 us
    all_to_all x5, waiting for transfers between devices, exchange(): return lax.all_to_all(rows, axes, split_axis=0, concat_axis=0, tiled=True)  52 us
    all_to_all x5, starting transfers between devices, exchange(): return lax.all_to_all(rows, axes, split_axis=0, concat_axis=0, tiled=True)  46.8 us
    pallas_call x1, Pallas kernels, local(): call_kernel(temporal_kernel, (BOTH_OUT, GAIN_OUT), 'temporal')  12 us
    pallas_call x1, Pallas kernels, local(): call_kernel(spatial_backward_kernel, (ROWS_OUT, GAIN_OUT), 'spatial_backw...  8.29 us
    pallas_call x1, Pallas kernels, local(): call_kernel(spatial_forward_kernel, (ROWS_OUT, MID_OUT, QKV_OUT), 'spatia...  8.05 us
    all_gather x2, waiting for transfers between devices, gather_weights(): full = lax.all_gather(part, 'rep', axis=0, tiled=False)  6.76 us
  transfers between devices with their start and end apart: 9, of which 7 were waited for; matrix products, arithmetic and copies ran while one was open for 7% of the time, Pallas kernels for 5%

profile of v4, /device:TPU:1, one launch (start us, length us, event | category | flops | bytes accessed | tf_op | source)
XLA Modules:
  0.0 253.0 jit_solution(6523720573785648214)
XLA Ops:
  7.2 0.7 convert_bitcast_fusion.2
  7.9 2.0 fusion.1
  9.9 0.9 dynamic-slice_bitcast_fusion.2
  10.8 0.8 dynamic-slice_bitcast_fusion
  11.9 1.2 broadcast_in_dim.20
  13.1 17.1 %all-to-all-start = ((bf16[64,2,2688]{2,1,0:T(2,128)(2,1)}), bf16[64,2,2688]{2,1,0:T(2,128)(2,1)S(1)}, u32[]{:S(2)}, u32[]{:S(2)}) async-start(bf16[64,2,2688]{2,1,0:T(2,128)(2,1)} %broadcast_in_dim.20), calls=%async_computation | async-start | bytes 1376256 | tf_op jit(solution)/shard_map/all_to_all | solution.py:332
  31.6 18.5 %all-to-all-done = bf16[64,2,2688]{2,1,0:T(2,128)(2,1)S(1)} async-done(((bf16[64,2,2688]{2,1,0:T(2,128)(2,1)}), bf16[64,2,2688]{2,1,0:T(2,128)(2,1)S(1)}, u32[]{:S(2)}, u32[]{:S(2)}) %all-to-all-start) | async-done | bytes 688160 | tf_op jit(solution)/shard_map/all_to_all | solution.py:332
  51.0 1.1 reshape.163
  52.5 1.0 maximum_maximum_fusion
  53.5 39.3 %all_to_all.35.got = bf16[64,4,2560]{2,1,0:T(4,128)(2,1)S(1)} all-to-all(bf16[64,4,2560]{2,1,0:T(4,128)(2,1)S(1)} %pad_maximum_fusion), channel_id=1, replica_groups=mesh['rep'=8,'z'=8,'y'=8] {'z','y'}, dimensions={0} | all-to-all | bytes 2621440 | tf_op jit(solution)/shard_map/all_to_all | solution.py:332
  94.4 1.1 reshape.168
  95.8 1.0 maximum_maximum_fusion.1
  97.0 0.7 slice.40
  98.2 3.1 %all-gather.11.cloned.1.call-done.full_hbm = bf16[1152,2304]{1,0:T(8,128)(2,1)} async-done(((bf16[144,2304]{1,0:T(8,128)(2,1)}), bf16[1152,2304]{1,0:T(8,128)(2,1)}) %all-gather.11.cloned.1.call-update) | async-done | bytes 5308432 | tf_op jit(solution)/shard_map/all_gather | solution.py:355
  101.3 8.0 %spatial_forward.1 = (bf16[256,1152]{1,0:T(8,128)(2,1)S(1)}, bf16[64,4,1152]{2,1,0:T(4,128)(2,1)}, bf16[3,576,256]{2,1,0:T(8,128)(2,1)S(1)}) custom-call(s32[4]{0:T(128)S(1)} %multiply_add_fusion.1.starts, bf16[2176,1152]{1,0:T(8,128)(2,1)} %all-gather.9.cloned.1.call-done.everyone, f32[3,1152]{1,0:T(4,128)S(1)} %copy-done.1, ...), custom_call_target="tpu_custom_call" | custom-call | flops 6000000000 | bytes 8000000 | tf_op jit(solution)/shard_map/spatial_forward/pallas_call | solution.py:422
  109.3 0.8 copy-done.2
  110.2 13.1 %all-to-all-start.2 = ((bf16[64,4,1152]{2,1,0:T(4,128)(2,1)}), bf16[64,4,1152]{2,1,0:T(4,128)(2,1)S(1)}, u32[]{:S(2)}, u32[]{:S(2)}) async-start(bf16[64,4,1152]{2,1,0:T(4,128)(2,1)} %get-tuple-element.13.mid), calls=%async_computation.2 | async-start | bytes 1179648 | tf_op jit(solution)/shard_map/all_to_all | solution.py:332
  124.2 17.8 %all-to-all-done.2.mid = bf16[64,4,1152]{2,1,0:T(4,128)(2,1)S(1)} async-done(((bf16[64,4,1152]{2,1,0:T(4,128)(2,1)}), bf16[64,4,1152]{2,1,0:T(4,128)(2,1)S(1)}, u32[]{:S(2)}, u32[]{:S(2)}) %all-to-all-start.2) | async-done | bytes 589856 | tf_op jit(solution)/shard_map/all_to_all | solution.py:332
  142.0 3.6 %all-gather.13.cloned.1.call-done.full_hbm = bf16[1152,2304]{1,0:T(8,128)(2,1)} async-done(((bf16[144,2304]{1,0:T(8,128)(2,1)}), bf16[1152,2304]{1,0:T(8,128)(2,1)}) %all-gather.13.cloned.1.call-update) | async-done | bytes 5308432 | tf_op jit(solution)/shard_map/all_gather | solution.py:355
  145.6 12.0 %temporal.1 = (bf16[64,4,1728]{2,1,0:T(4,128)(2,1)S(1)}, f32[3,1152]{1,0:T(4,128)S(1)}) custom-call(bf16[64,4,2560]{2,1,0:T(4,128)(2,1)S(1)} %all_to_all.35.got, bf16[64,4,1152]{2,1,0:T(4,128)(2,1)S(1)} %all-to-all-done.2.mid, f32[3,1152]{1,0:T(4,128)S(1)} %copy-done, bf16[1152,2304]{1,0:T(8,128)(2,1)} %all-gather.13.cloned.1.call-done.full_hbm, ...), custom_call_target="tpu_custom_call" | custom-call | flops 6000000000 | bytes 8000000 | tf_op jit(solution)/shard_map/temporal/pallas_call | solution.py:435
  157.6 37.9 %all_to_all.36.both = bf16[64,4,1728]{2,1,0:T(4,128)(2,1)S(1)} all-to-all(bf16[64,4,1728]{2,1,0:T(4,128)(2,1)S(1)} %get-tuple-element.15), channel_id=1, replica_groups=mesh['rep'=8,'z'=8,'y'=8] {'z','y'}, dimensions={0} | all-to-all | bytes 1769472 | tf_op jit(solution)/shard_map/all_to_all | solution.py:332
  195.6 8.3 %spatial_backward.1 = (bf16[256,1152]{1,0:T(8,128)(2,1)}, f32[3,1152]{1,0:T(4,128)S(1)}) custom-call(bf16[64,4,1728]{2,1,0:T(4,128)(2,1)S(1)} %all_to_all.36.both, bf16[256,1152]{1,0:T(8,128)(2,1)S(1)} %copy-done.3, f32[3,1152]{1,0:T(4,128)S(1)} %copy-done.1, bf16[1152,2304]{1,0:T(8,128)(2,1)} %all-gather.11.cloned.1.call-done.full_hbm, ...), custom_call_target="tpu_custom_call" | custom-call | flops 6000000000 | bytes 8000000 | tf_op jit(solution)/shard_map/spatial_backward/pallas_call | solution.py:439
  204.0 0.7 broadcast_in_dim.24
  204.6 5.2 %all-to-all-start.4 = ((bf16[8,54,128]{2,1,0:T(8,128)(2,1)}), bf16[8,54,128]{2,1,0:T(8,128)(2,1)S(1)}, u32[]{:S(2)}, u32[]{:S(2)}) async-start(bf16[8,54,128]{2,1,0:T(8,128)(2,1)} %broadcast_in_dim.24), calls=%async_computation.4 | async-start | bytes 229376 | tf_op jit(solution)/shard_map/all_to_all | solution.py:332
  210.1 7.5 %all-to-all-done.4 = bf16[8,54,128]{2,1,0:T(8,128)(2,1)S(1)} async-done(((bf16[8,54,128]{2,1,0:T(8,128)(2,1)}), bf16[8,54,128]{2,1,0:T(8,128)(2,1)S(1)}, u32[]{:S(2)}, u32[]{:S(2)}) %all-to-all-start.4) | async-done | bytes 110624 | tf_op jit(solution)/shard_map/all_to_all | solution.py:332
  217.6 0.7 broadcast_in_dim.25
  218.3 3.4 %all-to-all-start.5 = ((bf16[8,54,128]{2,1,0:T(8,128)(2,1)}), bf16[8,54,128]{2,1,0:T(8,128)(2,1)S(1)}, u32[]{:S(2)}, u32[]{:S(2)}) async-start(bf16[8,54,128]{2,1,0:T(8,128)(2,1)} %broadcast_in_dim.25), calls=%async_computation.5 | async-start | bytes 229376 | tf_op jit(solution)/shard_map/all_to_all | solution.py:332
  221.7 7.6 %all-to-all-done.5 = bf16[8,54,128]{2,1,0:T(8,128)(2,1)S(1)} async-done(((bf16[8,54,128]{2,1,0:T(8,128)(2,1)}), bf16[8,54,128]{2,1,0:T(8,128)(2,1)S(1)}, u32[]{:S(2)}, u32[]{:S(2)}) %all-to-all-start.5) | async-done | bytes 110624 | tf_op jit(solution)/shard_map/all_to_all | solution.py:332
  229.3 0.7 broadcast_in_dim.26
  230.0 8.0 %all-to-all-start.6 = ((bf16[8,54,128]{2,1,0:T(8,128)(2,1)}), bf16[8,54,128]{2,1,0:T(8,128)(2,1)S(1)}, u32[]{:S(2)}, u32[]{:S(2)}) async-start(bf16[8,54,128]{2,1,0:T(8,128)(2,1)} %broadcast_in_dim.26), calls=%async_computation.6 | async-start | bytes 229376 | tf_op jit(solution)/shard_map/all_to_all | solution.py:332
  238.0 4.5 %finish.1 = bf16[256,1152]{1,0:T(8,128)(2,1)} custom-call(bf16[64,4,1152]{2,1,0:T(4,128)(2,1)} %get-tuple-element.13.mid, bf16[64,4,1728]{2,1,0:T(4,128)(2,1)S(1)} %all_to_all.36.both, bf16[1152,2304]{1,0:T(8,128)(2,1)} %all-gather.13.cloned.1.call-done.full_hbm), custom_call_target="tpu_custom_call" | custom-call | flops 6000000000 | bytes 8000000 | tf_op jit(solution)/shard_map/finish/pallas_call | solution.py:442
  243.9 2.5 pick.1
  (81 shorter events, 8.1 us)
Async XLA Ops:
  7.2 89.9 %all-gather.9.cloned.1.call-start = ((), (), s32[]{:S(2)}) async-start(), calls=%async_computation.7 | async-start | bytes 5640192 | tf_op jit(solution)/shard_map/all_gather | solution.py:384
  9.8 20.8 %copy-start.4 = (bf16[4,1,64,1152]{3,2,1,0:T(8,128)(2,1)S(1)}, bf16[4,1,64,1152]{3,2,1,0:T(8,128)(2,1)}, u32[]{:S(2)}) copy-start(bf16[4,1,64,1152]{3,2,1,0:T(8,128)(2,1)} %param.21) | copy-start | bytes 1769476
  13.1 37.0 %all-to-all-start = ((bf16[64,2,2688]{2,1,0:T(2,128)(2,1)}), bf16[64,2,2688]{2,1,0:T(2,128)(2,1)S(1)}, u32[]{:S(2)}, u32[]{:S(2)}) async-start(bf16[64,2,2688]{2,1,0:T(2,128)(2,1)} %broadcast_in_dim.20), calls=%async_computation | async-start | bytes 1376256 | tf_op jit(solution)/shard_map/all_to_all | solution.py:332
  30.2 71.0 %all-gather.11.cloned.1.call-start = ((), (), s32[]{:S(2)}) async-start(), calls=%async_computation.8 | async-start | bytes 5971968 | tf_op jit(solution)/shard_map/all_gather | solution.py:355
  53.5 92.1 %all-gather.13.cloned.1.call-start = ((), (), s32[]{:S(2)}) async-start(), calls=%async_computation.9 | async-start | bytes 5971968 | tf_op jit(solution)/shard_map/all_gather | solution.py:355
  95.7 1.1 copy-start.6
  95.7 5.5 %copy-start.1 = (f32[3,1152]{1,0:T(4,128)S(1)}, f32[3,1152]{1,0:T(4,128)}, u32[]{:S(2)}) copy-start(f32[3,1152]{1,0:T(4,128)} %gains.5) | copy-start | bytes 41476
  98.1 25.4 %copy-start.5 = (s32[4,4]{1,0:T(4,128)S(1)}, s32[4,4]{1,0:T(4,128)}, u32[]{:S(2)}) copy-start(s32[4,4]{1,0:T(4,128)} %param.14) | copy-start | bytes 196
  109.3 0.8 copy-start.2
  110.2 35.4 %copy-start = (f32[3,1152]{1,0:T(4,128)S(1)}, f32[3,1152]{1,0:T(4,128)}, u32[]{:S(2)}) copy-start(f32[3,1152]{1,0:T(4,128)} %gains.4) | copy-start | bytes 41476
  110.2 31.8 %all-to-all-start.2 = ((bf16[64,4,1152]{2,1,0:T(4,128)(2,1)}), bf16[64,4,1152]{2,1,0:T(4,128)(2,1)S(1)}, u32[]{:S(2)}, u32[]{:S(2)}) async-start(bf16[64,4,1152]{2,1,0:T(4,128)(2,1)} %get-tuple-element.13.mid), calls=%async_computation.2 | async-start | bytes 1179648 | tf_op jit(solution)/shard_map/all_to_all | solution.py:332
  123.3 120.6 %all-gather.15.cloned.1.call-start = ((), (), s32[]{:S(2)}) async-start(), calls=%async_computation.10 | async-start | bytes 5308416 | tf_op jit(solution)/shard_map/all_gather | solution.py:443
  157.6 38.0 %copy-start.3 = (bf16[256,1152]{1,0:T(8,128)(2,1)S(1)}, bf16[256,1152]{1,0:T(8,128)(2,1)}, u32[]{:S(2)}) copy-start(bf16[256,1152]{1,0:T(8,128)(2,1)} %copy-done.2) | copy-start | bytes 1769476
  195.6 14.3 %copy-start.7 = (s32[4]{0:T(128)S(1)}, s32[4]{0:T(128)}, u32[]{:S(2)}) copy-start(s32[4]{0:T(128)} %param.12) | copy-start | bytes 52
  204.6 12.9 %all-to-all-start.4 = ((bf16[8,54,128]{2,1,0:T(8,128)(2,1)}), bf16[8,54,128]{2,1,0:T(8,128)(2,1)S(1)}, u32[]{:S(2)}, u32[]{:S(2)}) async-start(bf16[8,54,128]{2,1,0:T(8,128)(2,1)} %broadcast_in_dim.24), calls=%async_computation.4 | async-start | bytes 229376 | tf_op jit(solution)/shard_map/all_to_all | solution.py:332
  218.3 11.0 %all-to-all-start.5 = ((bf16[8,54,128]{2,1,0:T(8,128)(2,1)}), bf16[8,54,128]{2,1,0:T(8,128)(2,1)S(1)}, u32[]{:S(2)}, u32[]{:S(2)}) async-start(bf16[8,54,128]{2,1,0:T(8,128)(2,1)} %broadcast_in_dim.25), calls=%async_computation.5 | async-start | bytes 229376 | tf_op jit(solution)/shard_map/all_to_all | solution.py:332
  230.0 13.2 %all-to-all-start.6 = ((bf16[8,54,128]{2,1,0:T(8,128)(2,1)}), bf16[8,54,128]{2,1,0:T(8,128)(2,1)S(1)}, u32[]{:S(2)}, u32[]{:S(2)}) async-start(bf16[8,54,128]{2,1,0:T(8,128)(2,1)} %broadcast_in_dim.26), calls=%async_computation.6 | async-start | bytes 229376 | tf_op jit(solution)/shard_map/all_to_all | solution.py:332
Sparse Core Ops, SparseCore 0:
  10.1 46.7 all-gather.8
  59.0 42.1 all-gather.10
  103.4 42.1 all-gather.12
  204.0 35.5 all-gather.14

commit v5 on v4

--- a/solution.py
+++ b/solution.py
@@ -446,8 +446,12 @@
     )
     sums = jnp.stack([grad_spatial, grad_temporal]).reshape(-1, 128)
     for axis in ("y", "z", "rep"):
-        sent = sums.astype(jnp.bfloat16)
-        sums = jnp.sum(spread(sent, axis).astype(jnp.float32), axis=0)
+        got = spread(sums.astype(jnp.bfloat16), axis)
+        if axis == "y":
+            got, block_out = lax.optimization_barrier((got, block_out))
+        if axis == "rep":
+            got, latent_grad = lax.optimization_barrier((got, latent_grad))
+        sums = jnp.sum(got.astype(jnp.float32), axis=0)
     gain_grads = sums.reshape((2,) + gains_spatial.shape)
     return (block_out.reshape(latents.shape), latent_grad.reshape(latents.shape), gain_grads)
 

time: 254 us -> 252 us (level)
    all_to_all x5, waiting for transfers between devices: 52 us -> 48.4 us  [exchange(): return lax.all_to_all(rows, axes, split_axis=0, concat_axis=0, tiled=True)]
  transfers between devices with their start and end apart: 9 -> 9, of which waited for: 7 -> 8; matrix products, arithmetic and copies ran while one was open for 7% -> 6% of each run, Pallas kernels for 5% -> 6%
where the time goes in v5:
time: 252 us; the launch traced here: 251 us
  blocking collectives  77.2 us (31%)
  waiting for transfers between devices  56.6 us (22%)
  starting transfers between devices  47.2 us (19%)
  Pallas kernels  35.3 us (14%)
  between operations  14.1 us (6%)
  local copies, waits for them, and re-layouts  13.8 us (5%)
  other arithmetic  6.35 us (3%)
    all_to_all x2, blocking collectives, exchange(): return lax.all_to_all(rows, axes, split_axis=0, concat_axis=0, tiled=True)  77.2 us
    all_to_all x5, waiting for transfers between devices, exchange(): return lax.all_to_all(rows, axes, split_axis=0, concat_axis=0, tiled=True)  48.4 us
    all_to_all x5, starting transfers between devices, exchange(): return lax.all_to_all(rows, axes, split_axis=0, concat_axis=0, tiled=True)  46.8 us
    pallas_call x1, Pallas kernels, local(): call_kernel(temporal_kernel, (BOTH_OUT, GAIN_OUT), 'temporal')  12 us
    pallas_call x1, Pallas kernels, local(): call_kernel(spatial_backward_kernel, (ROWS_OUT, GAIN_OUT), 'spatial_backw...  8.28 us
    pallas_call x1, Pallas kernels, local(): call_kernel(spatial_forward_kernel, (ROWS_OUT, MID_OUT, QKV_OUT), 'spatia...  8.03 us
    all_gather x2, waiting for transfers between devices, gather_weights(): full = lax.all_gather(part, 'rep', axis=0, tiled=False)  6.76 us
  transfers between devices with their start and end apart: 9, of which 8 were waited for; matrix products, arithmetic and copies ran while one was open for 6% of the time, Pallas kernels for 6%

profile of v5, /device:TPU:1, one launch (start us, length us, event | category | flops | bytes accessed | tf_op | source)
XLA Modules:
  0.0 250.6 jit_solution(14336796659829327613)
XLA Ops:
  7.2 0.7 convert_bitcast_fusion.2
  7.9 2.0 fusion.1
  9.9 0.9 dynamic-slice_bitcast_fusion.2
  10.8 0.8 dynamic-slice_bitcast_fusion
  11.9 1.2 broadcast_in_dim.19
  13.1 17.1 %all-to-all-start = ((bf16[64,2,2688]{2,1,0:T(2,128)(2,1)}), bf16[64,2,2688]{2,1,0:T(2,128)(2,1)S(1)}, u32[]{:S(2)}, u32[]{:S(2)}) async-start(bf16[64,2,2688]{2,1,0:T(2,128)(2,1)} %broadcast_in_dim.19), calls=%async_computation | async-start | bytes 1376256 | tf_op jit(solution)/shard_map/all_to_all | solution.py:332
  31.6 18.5 %all-to-all-done = bf16[64,2,2688]{2,1,0:T(2,128)(2,1)S(1)} async-done(((bf16[64,2,2688]{2,1,0:T(2,128)(2,1)}), bf16[64,2,2688]{2,1,0:T(2,128)(2,1)S(1)}, u32[]{:S(2)}, u32[]{:S(2)}) %all-to-all-start) | async-done | bytes 688160 | tf_op jit(solution)/shard_map/all_to_all | solution.py:332
  51.0 1.1 reshape.163
  52.5 1.0 maximum_maximum_fusion
  53.5 39.3 %all_to_all.35.got = bf16[64,4,2560]{2,1,0:T(4,128)(2,1)S(1)} all-to-all(bf16[64,4,2560]{2,1,0:T(4,128)(2,1)S(1)} %pad_maximum_fusion), channel_id=1, replica_groups=mesh['rep'=8,'z'=8,'y'=8] {'z','y'}, dimensions={0} | all-to-all | bytes 2621440 | tf_op jit(solution)/shard_map/all_to_all | solution.py:332
  94.4 1.1 reshape.168
  95.8 1.0 maximum_maximum_fusion.1
  97.0 0.7 slice.40
  98.2 3.1 %all-gather.11.cloned.1.call-done.full_hbm = bf16[1152,2304]{1,0:T(8,128)(2,1)} async-done(((bf16[144,2304]{1,0:T(8,128)(2,1)}), bf16[1152,2304]{1,0:T(8,128)(2,1)}) %all-gather.11.cloned.1.call-update) | async-done | bytes 5308432 | tf_op jit(solution)/shard_map/all_gather | solution.py:355
  101.3 8.0 %spatial_forward.1 = (bf16[256,1152]{1,0:T(8,128)(2,1)S(1)}, bf16[64,4,1152]{2,1,0:T(4,128)(2,1)}, bf16[3,576,256]{2,1,0:T(8,128)(2,1)S(1)}) custom-call(s32[4]{0:T(128)S(1)} %multiply_add_fusion.1.starts, bf16[2176,1152]{1,0:T(8,128)(2,1)} %all-gather.9.cloned.1.call-done.everyone, f32[3,1152]{1,0:T(4,128)S(1)} %copy-done.1, ...), custom_call_target="tpu_custom_call" | custom-call | flops 6000000000 | bytes 8000000 | tf_op jit(solution)/shard_map/spatial_forward/pallas_call | solution.py:422
  109.3 0.8 copy-done.2
  110.1 13.1 %all-to-all-start.2 = ((bf16[64,4,1152]{2,1,0:T(4,128)(2,1)}), bf16[64,4,1152]{2,1,0:T(4,128)(2,1)S(1)}, u32[]{:S(2)}, u32[]{:S(2)}) async-start(bf16[64,4,1152]{2,1,0:T(4,128)(2,1)} %get-tuple-element.18.mid), calls=%async_computation.2 | async-start | bytes 1179648 | tf_op jit(solution)/shard_map/all_to_all | solution.py:332
  124.2 17.8 %all-to-all-done.2.mid = bf16[64,4,1152]{2,1,0:T(4,128)(2,1)S(1)} async-done(((bf16[64,4,1152]{2,1,0:T(4,128)(2,1)}), bf16[64,4,1152]{2,1,0:T(4,128)(2,1)S(1)}, u32[]{:S(2)}, u32[]{:S(2)}) %all-to-all-start.2) | async-done | bytes 589856 | tf_op jit(solution)/shard_map/all_to_all | solution.py:332
  142.0 3.6 %all-gather.13.cloned.1.call-done.full_hbm = bf16[1152,2304]{1,0:T(8,128)(2,1)} async-done(((bf16[144,2304]{1,0:T(8,128)(2,1)}), bf16[1152,2304]{1,0:T(8,128)(2,1)}) %all-gather.13.cloned.1.call-update) | async-done | bytes 5308432 | tf_op jit(solution)/shard_map/all_gather | solution.py:355
  145.6 12.0 %temporal.1 = (bf16[64,4,1728]{2,1,0:T(4,128)(2,1)S(1)}, f32[3,1152]{1,0:T(4,128)S(1)}) custom-call(bf16[64,4,2560]{2,1,0:T(4,128)(2,1)S(1)} %all_to_all.35.got, bf16[64,4,1152]{2,1,0:T(4,128)(2,1)S(1)} %all-to-all-done.2.mid, f32[3,1152]{1,0:T(4,128)S(1)} %copy-done, bf16[1152,2304]{1,0:T(8,128)(2,1)} %all-gather.13.cloned.1.call-done.full_hbm, ...), custom_call_target="tpu_custom_call" | custom-call | flops 6000000000 | bytes 8000000 | tf_op jit(solution)/shard_map/temporal/pallas_call | solution.py:435
  157.6 37.9 %all_to_all.36.both = bf16[64,4,1728]{2,1,0:T(4,128)(2,1)S(1)} all-to-all(bf16[64,4,1728]{2,1,0:T(4,128)(2,1)S(1)} %get-tuple-element.19), channel_id=1, replica_groups=mesh['rep'=8,'z'=8,'y'=8] {'z','y'}, dimensions={0} | all-to-all | bytes 1769472 | tf_op jit(solution)/shard_map/all_to_all | solution.py:332
  195.6 8.3 %spatial_backward.1 = (bf16[256,1152]{1,0:T(8,128)(2,1)}, f32[3,1152]{1,0:T(4,128)S(1)}) custom-call(bf16[64,4,1728]{2,1,0:T(4,128)(2,1)S(1)} %all_to_all.36.both, bf16[256,1152]{1,0:T(8,128)(2,1)S(1)} %copy-done.3, f32[3,1152]{1,0:T(4,128)S(1)} %copy-done.1, bf16[1152,2304]{1,0:T(8,128)(2,1)} %all-gather.11.cloned.1.call-done.full_hbm, ...), custom_call_target="tpu_custom_call" | custom-call | flops 6000000000 | bytes 8000000 | tf_op jit(solution)/shard_map/spatial_backward/pallas_call | solution.py:439
  204.9 5.2 %all-to-all-start.4 = ((bf16[8,54,128]{2,1,0:T(8,128)(2,1)}), bf16[8,54,128]{2,1,0:T(8,128)(2,1)S(1)}, u32[]{:S(2)}, u32[]{:S(2)}) async-start(bf16[8,54,128]{2,1,0:T(8,128)(2,1)} %broadcast_in_dim.24), calls=%async_computation.4 | async-start | bytes 229376 | tf_op jit(solution)/shard_map/all_to_all | solution.py:332
  210.1 4.5 %finish.1 = bf16[256,1152]{1,0:T(8,128)(2,1)} custom-call(bf16[64,4,1152]{2,1,0:T(4,128)(2,1)} %get-tuple-element.18.mid, bf16[64,4,1728]{2,1,0:T(4,128)(2,1)S(1)} %all_to_all.36.both, bf16[1152,2304]{1,0:T(8,128)(2,1)} %all-gather.13.cloned.1.call-done.full_hbm), custom_call_target="tpu_custom_call" | custom-call | flops 6000000000 | bytes 8000000 | tf_op jit(solution)/shard_map/finish/pallas_call | solution.py:442
  214.5 3.3 %all-to-all-done.4 = bf16[8,54,128]{2,1,0:T(8,128)(2,1)S(1)} async-done(((bf16[8,54,128]{2,1,0:T(8,128)(2,1)}), bf16[8,54,128]{2,1,0:T(8,128)(2,1)S(1)}, u32[]{:S(2)}, u32[]{:S(2)}) %all-to-all-start.4) | async-done | bytes 110624 | tf_op jit(solution)/shard_map/all_to_all | solution.py:332
  217.8 0.7 broadcast_in_dim.25
  218.5 3.4 %all-to-all-start.5 = ((bf16[8,54,128]{2,1,0:T(8,128)(2,1)}), bf16[8,54,128]{2,1,0:T(8,128)(2,1)S(1)}, u32[]{:S(2)}, u32[]{:S(2)}) async-start(bf16[8,54,128]{2,1,0:T(8,128)(2,1)} %broadcast_in_dim.25), calls=%async_computation.5 | async-start | bytes 229376 | tf_op jit(solution)/shard_map/all_to_all | solution.py:332
  221.9 7.6 %all-to-all-done.5 = bf16[8,54,128]{2,1,0:T(8,128)(2,1)S(1)} async-done(((bf16[8,54,128]{2,1,0:T(8,128)(2,1)}), bf16[8,54,128]{2,1,0:T(8,128)(2,1)S(1)}, u32[]{:S(2)}, u32[]{:S(2)}) %all-to-all-start.5) | async-done | bytes 110624 | tf_op jit(solution)/shard_map/all_to_all | solution.py:332
  230.2 8.0 %all-to-all-start.6 = ((bf16[8,54,128]{2,1,0:T(8,128)(2,1)}), bf16[8,54,128]{2,1,0:T(8,128)(2,1)S(1)}, u32[]{:S(2)}, u32[]{:S(2)}) async-start(bf16[8,54,128]{2,1,0:T(8,128)(2,1)} %broadcast_in_dim.26), calls=%async_computation.6 | async-start | bytes 229376 | tf_op jit(solution)/shard_map/all_to_all | solution.py:332
  238.3 1.4 all-gather.15.cloned.1.call-done.everyone
  239.6 2.5 %pick.1 = bf16[256,1152]{1,0:T(8,128)(2,1)} custom-call(s32[4]{0:T(128)S(1)} %multiply_add_fusion.starts, bf16[2048,1152]{1,0:T(8,128)(2,1)} %all-gather.15.cloned.1.call-done.everyone), custom_call_target="tpu_custom_call" | custom-call | flops 6000000000 | bytes 8000000 | tf_op jit(solution)/shard_map/pick/pallas_call | solution.py:444
  242.1 1.3 all-to-all-done.6
  (81 shorter events, 8.7 us)
Async XLA Ops:
  7.2 89.9 %all-gather.9.cloned.1.call-start = ((), (), s32[]{:S(2)}) async-start(), calls=%async_computation.7 | async-start | bytes 5640192 | tf_op jit(solution)/shard_map/all_gather | solution.py:384
  9.8 20.8 %copy-start.4 = (bf16[4,1,64,1152]{3,2,1,0:T(8,128)(2,1)S(1)}, bf16[4,1,64,1152]{3,2,1,0:T(8,128)(2,1)}, u32[]{:S(2)}) copy-start(bf16[4,1,64,1152]{3,2,1,0:T(8,128)(2,1)} %param.21) | copy-start | bytes 1769476
  13.1 37.0 %all-to-all-start = ((bf16[64,2,2688]{2,1,0:T(2,128)(2,1)}), bf16[64,2,2688]{2,1,0:T(2,128)(2,1)S(1)}, u32[]{:S(2)}, u32[]{:S(2)}) async-start(bf16[64,2,2688]{2,1,0:T(2,128)(2,1)} %broadcast_in_dim.19), calls=%async_computation | async-start | bytes 1376256 | tf_op jit(solution)/shard_map/all_to_all | solution.py:332
  30.2 71.0 %all-gather.11.cloned.1.call-start = ((), (), s32[]{:S(2)}) async-start(), calls=%async_computation.8 | async-start | bytes 5971968 | tf_op jit(solution)/shard_map/all_gather | solution.py:355
  53.5 92.1 %all-gather.13.cloned.1.call-start = ((), (), s32[]{:S(2)}) async-start(), calls=%async_computation.9 | async-start | bytes 5971968 | tf_op jit(solution)/shard_map/all_gather | solution.py:355
  95.7 1.1 copy-start.6
  95.7 5.5 %copy-start.1 = (f32[3,1152]{1,0:T(4,128)S(1)}, f32[3,1152]{1,0:T(4,128)}, u32[]{:S(2)}) copy-start(f32[3,1152]{1,0:T(4,128)} %gains.5) | copy-start | bytes 41476
  98.1 25.4 %copy-start.5 = (s32[4,4]{1,0:T(4,128)S(1)}, s32[4,4]{1,0:T(4,128)}, u32[]{:S(2)}) copy-start(s32[4,4]{1,0:T(4,128)} %param.14) | copy-start | bytes 196
  109.3 0.8 copy-start.2
  110.1 35.5 %copy-start = (f32[3,1152]{1,0:T(4,128)S(1)}, f32[3,1152]{1,0:T(4,128)}, u32[]{:S(2)}) copy-start(f32[3,1152]{1,0:T(4,128)} %gains.4) | copy-start | bytes 41476
  110.1 31.8 %all-to-all-start.2 = ((bf16[64,4,1152]{2,1,0:T(4,128)(2,1)}), bf16[64,4,1152]{2,1,0:T(4,128)(2,1)S(1)}, u32[]{:S(2)}, u32[]{:S(2)}) async-start(bf16[64,4,1152]{2,1,0:T(4,128)(2,1)} %get-tuple-element.18.mid), calls=%async_computation.2 | async-start | bytes 1179648 | tf_op jit(solution)/shard_map/all_to_all | solution.py:332
  123.3 116.3 %all-gather.15.cloned.1.call-start = ((), (), s32[]{:S(2)}) async-start(), calls=%async_computation.10 | async-start | bytes 5308416 | tf_op jit(solution)/shard_map/all_gather | solution.py:443
  157.6 38.0 %copy-start.3 = (bf16[256,1152]{1,0:T(8,128)(2,1)S(1)}, bf16[256,1152]{1,0:T(8,128)(2,1)}, u32[]{:S(2)}) copy-start(bf16[256,1152]{1,0:T(8,128)(2,1)} %copy-done.2) | copy-start | bytes 1769476
  195.6 8.3 %copy-start.7 = (s32[4]{0:T(128)S(1)}, s32[4]{0:T(128)}, u32[]{:S(2)}) copy-start(s32[4]{0:T(128)} %param.12) | copy-start | bytes 52
  204.9 12.9 %all-to-all-start.4 = ((bf16[8,54,128]{2,1,0:T(8,128)(2,1)}), bf16[8,54,128]{2,1,0:T(8,128)(2,1)S(1)}, u32[]{:S(2)}, u32[]{:S(2)}) async-start(bf16[8,54,128]{2,1,0:T(8,128)(2,1)} %broadcast_in_dim.24), calls=%async_computation.4 | async-start | bytes 229376 | tf_op jit(solution)/shard_map/all_to_all | solution.py:332
  218.5 11.0 %all-to-all-start.5 = ((bf16[8,54,128]{2,1,0:T(8,128)(2,1)}), bf16[8,54,128]{2,1,0:T(8,128)(2,1)S(1)}, u32[]{:S(2)}, u32[]{:S(2)}) async-start(bf16[8,54,128]{2,1,0:T(8,128)(2,1)} %broadcast_in_dim.25), calls=%async_computation.5 | async-start | bytes 229376 | tf_op jit(solution)/shard_map/all_to_all | solution.py:332
  230.2 13.2 %all-to-all-start.6 = ((bf16[8,54,128]{2,1,0:T(8,128)(2,1)}), bf16[8,54,128]{2,1,0:T(8,128)(2,1)S(1)}, u32[]{:S(2)}, u32[]{:S(2)}) async-start(bf16[8,54,128]{2,1,0:T(8,128)(2,1)} %broadcast_in_dim.26), calls=%async_computation.6 | async-start | bytes 229376 | tf_op jit(solution)/shard_map/all_to_all | solution.py:332
Sparse Core Ops, SparseCore 0:
  10.1 46.7 all-gather.8
  59.0 42.1 all-gather.10
  103.4 42.1 all-gather.12
  204.0 35.5 all-gather.14

commit v6 on v5

--- a/solution.py
+++ b/solution.py
@@ -223,13 +223,15 @@
     full, sems, u, q, k, x, o, dq, dk, dx, g,
 ):
     copies = weight_copies(full_hbm, full, sems)
-    for copy in copies[::-1]:
+    for copy in copies[2:]:
         copy.start()
     for which, ref in enumerate((q, k, x)):
         ref[...] = qkv[which].astype(jnp.float32)
     g[...] = both[:, :, :1152].reshape(g.shape)
-    copies[3].wait()
-    copies[2].wait()
+    for copy in copies[2:]:
+        copy.wait()
+    for copy in copies[:2]:
+        copy.start()
     load_u(full, u)
     backward(
         g, v, gains, full, copies[:2], valid_keys(counts), grad, gain,

time: 252 us -> 252 us (level)
  no operation moved by 1% of the time
where the time goes in v6:
time: 252 us; the launch traced here: 251 us
  blocking collectives  77.2 us (31%)
  waiting for transfers between devices  56.6 us (22%)
  starting transfers between devices  47.2 us (19%)
  Pallas kernels  35.3 us (14%)
  between operations  14.1 us (6%)
  local copies, waits for them, and re-layouts  13.8 us (5%)
  other arithmetic  6.35 us (3%)
    all_to_all x2, blocking collectives, exchange(): return lax.all_to_all(rows, axes, split_axis=0, concat_axis=0, tiled=True)  77.2 us
    all_to_all x5, waiting for transfers between devices, exchange(): return lax.all_to_all(rows, axes, split_axis=0, concat_axis=0, tiled=True)  48.4 us
    all_to_all x5, starting transfers between devices, exchange(): return lax.all_to_all(rows, axes, split_axis=0, concat_axis=0, tiled=True)  46.8 us
    pallas_call x1, Pallas kernels, local(): call_kernel(temporal_kernel, (BOTH_OUT, GAIN_OUT), 'temporal')  12 us
    pallas_call x1, Pallas kernels, local(): call_kernel(spatial_backward_kernel, (ROWS_OUT, GAIN_OUT), 'spatial_backw...  8.27 us
    pallas_call x1, Pallas kernels, local(): call_kernel(spatial_forward_kernel, (ROWS_OUT, MID_OUT, QKV_OUT), 'spatia...  8.03 us
    all_gather x2, waiting for transfers between devices, gather_weights(): full = lax.all_gather(part, 'rep', axis=0, tiled=False)  6.76 us
  transfers between devices with their start and end apart: 9, of which 8 were waited for; matrix products, arithmetic and copies ran while one was open for 6% of the time, Pallas kernels for 6%

profile of v6, /device:TPU:1, one launch (start us, length us, event | category | flops | bytes accessed | tf_op | source)
XLA Modules:
  0.0 250.6 jit_solution(17426495596445294033)
XLA Ops:
  7.2 0.7 convert_bitcast_fusion.2
  7.9 2.0 fusion.1
  9.9 0.9 dynamic-slice_bitcast_fusion.2
  10.8 0.8 dynamic-slice_bitcast_fusion
  11.9 1.2 broadcast_in_dim.19
  13.1 17.1 %all-to-all-start = ((bf16[64,2,2688]{2,1,0:T(2,128)(2,1)}), bf16[64,2,2688]{2,1,0:T(2,128)(2,1)S(1)}, u32[]{:S(2)}, u32[]{:S(2)}) async-start(bf16[64,2,2688]{2,1,0:T(2,128)(2,1)} %broadcast_in_dim.19), calls=%async_computation | async-start | bytes 1376256 | tf_op jit(solution)/shard_map/all_to_all | solution.py:334
  31.6 18.5 %all-to-all-done = bf16[64,2,2688]{2,1,0:T(2,128)(2,1)S(1)} async-done(((bf16[64,2,2688]{2,1,0:T(2,128)(2,1)}), bf16[64,2,2688]{2,1,0:T(2,128)(2,1)S(1)}, u32[]{:S(2)}, u32[]{:S(2)}) %all-to-all-start) | async-done | bytes 688160 | tf_op jit(solution)/shard_map/all_to_all | solution.py:334
  51.0 1.1 reshape.163
  52.5 1.0 maximum_maximum_fusion
  53.5 39.3 %all_to_all.35.got = bf16[64,4,2560]{2,1,0:T(4,128)(2,1)S(1)} all-to-all(bf16[64,4,2560]{2,1,0:T(4,128)(2,1)S(1)} %pad_maximum_fusion), channel_id=1, replica_groups=mesh['rep'=8,'z'=8,'y'=8] {'z','y'}, dimensions={0} | all-to-all | bytes 2621440 | tf_op jit(solution)/shard_map/all_to_all | solution.py:334
  94.4 1.1 reshape.168
  95.8 1.0 maximum_maximum_fusion.1
  97.0 0.7 slice.40
  98.2 3.1 %all-gather.11.cloned.1.call-done.full_hbm = bf16[1152,2304]{1,0:T(8,128)(2,1)} async-done(((bf16[144,2304]{1,0:T(8,128)(2,1)}), bf16[1152,2304]{1,0:T(8,128)(2,1)}) %all-gather.11.cloned.1.call-update) | async-done | bytes 5308432 | tf_op jit(solution)/shard_map/all_gather | solution.py:357
  101.3 8.0 %spatial_forward.1 = (bf16[256,1152]{1,0:T(8,128)(2,1)S(1)}, bf16[64,4,1152]{2,1,0:T(4,128)(2,1)}, bf16[3,576,256]{2,1,0:T(8,128)(2,1)S(1)}) custom-call(s32[4]{0:T(128)S(1)} %multiply_add_fusion.1.starts, bf16[2176,1152]{1,0:T(8,128)(2,1)} %all-gather.9.cloned.1.call-done.everyone, f32[3,1152]{1,0:T(4,128)S(1)} %copy-done.1, ...), custom_call_target="tpu_custom_call" | custom-call | flops 6000000000 | bytes 8000000 | tf_op jit(solution)/shard_map/spatial_forward/pallas_call | solution.py:424
  109.3 0.8 copy-done.2
  110.1 13.1 %all-to-all-start.2 = ((bf16[64,4,1152]{2,1,0:T(4,128)(2,1)}), bf16[64,4,1152]{2,1,0:T(4,128)(2,1)S(1)}, u32[]{:S(2)}, u32[]{:S(2)}) async-start(bf16[64,4,1152]{2,1,0:T(4,128)(2,1)} %get-tuple-element.18.mid), calls=%async_computation.2 | async-start | bytes 1179648 | tf_op jit(solution)/shard_map/all_to_all | solution.py:334
  124.2 17.8 %all-to-all-done.2.mid = bf16[64,4,1152]{2,1,0:T(4,128)(2,1)S(1)} async-done(((bf16[64,4,1152]{2,1,0:T(4,128)(2,1)}), bf16[64,4,1152]{2,1,0:T(4,128)(2,1)S(1)}, u32[]{:S(2)}, u32[]{:S(2)}) %all-to-all-start.2) | async-done | bytes 589856 | tf_op jit(solution)/shard_map/all_to_all | solution.py:334
  142.0 3.6 %all-gather.13.cloned.1.call-done.full_hbm = bf16[1152,2304]{1,0:T(8,128)(2,1)} async-done(((bf16[144,2304]{1,0:T(8,128)(2,1)}), bf16[1152,2304]{1,0:T(8,128)(2,1)}) %all-gather.13.cloned.1.call-update) | async-done | bytes 5308432 | tf_op jit(solution)/shard_map/all_gather | solution.py:357
  145.6 12.0 %temporal.1 = (bf16[64,4,1728]{2,1,0:T(4,128)(2,1)S(1)}, f32[3,1152]{1,0:T(4,128)S(1)}) custom-call(bf16[64,4,2560]{2,1,0:T(4,128)(2,1)S(1)} %all_to_all.35.got, bf16[64,4,1152]{2,1,0:T(4,128)(2,1)S(1)} %all-to-all-done.2.mid, f32[3,1152]{1,0:T(4,128)S(1)} %copy-done, bf16[1152,2304]{1,0:T(8,128)(2,1)} %all-gather.13.cloned.1.call-done.full_hbm, ...), custom_call_target="tpu_custom_call" | custom-call | flops 6000000000 | bytes 8000000 | tf_op jit(solution)/shard_map/temporal/pallas_call | solution.py:437
  157.6 37.9 %all_to_all.36.both = bf16[64,4,1728]{2,1,0:T(4,128)(2,1)S(1)} all-to-all(bf16[64,4,1728]{2,1,0:T(4,128)(2,1)S(1)} %get-tuple-element.19), channel_id=1, replica_groups=mesh['rep'=8,'z'=8,'y'=8] {'z','y'}, dimensions={0} | all-to-all | bytes 1769472 | tf_op jit(solution)/shard_map/all_to_all | solution.py:334
  195.6 8.3 %spatial_backward.1 = (bf16[256,1152]{1,0:T(8,128)(2,1)}, f32[3,1152]{1,0:T(4,128)S(1)}) custom-call(bf16[64,4,1728]{2,1,0:T(4,128)(2,1)S(1)} %all_to_all.36.both, bf16[256,1152]{1,0:T(8,128)(2,1)S(1)} %copy-done.3, f32[3,1152]{1,0:T(4,128)S(1)} %copy-done.1, bf16[1152,2304]{1,0:T(8,128)(2,1)} %all-gather.11.cloned.1.call-done.full_hbm, ...), custom_call_target="tpu_custom_call" | custom-call | flops 6000000000 | bytes 8000000 | tf_op jit(solution)/shard_map/spatial_backward/pallas_call | solution.py:441
  204.9 5.2 %all-to-all-start.4 = ((bf16[8,54,128]{2,1,0:T(8,128)(2,1)}), bf16[8,54,128]{2,1,0:T(8,128)(2,1)S(1)}, u32[]{:S(2)}, u32[]{:S(2)}) async-start(bf16[8,54,128]{2,1,0:T(8,128)(2,1)} %broadcast_in_dim.24), calls=%async_computation.4 | async-start | bytes 229376 | tf_op jit(solution)/shard_map/all_to_all | solution.py:334
  210.1 4.5 %finish.1 = bf16[256,1152]{1,0:T(8,128)(2,1)} custom-call(bf16[64,4,1152]{2,1,0:T(4,128)(2,1)} %get-tuple-element.18.mid, bf16[64,4,1728]{2,1,0:T(4,128)(2,1)S(1)} %all_to_all.36.both, bf16[1152,2304]{1,0:T(8,128)(2,1)} %all-gather.13.cloned.1.call-done.full_hbm), custom_call_target="tpu_custom_call" | custom-call | flops 6000000000 | bytes 8000000 | tf_op jit(solution)/shard_map/finish/pallas_call | solution.py:444
  214.5 3.3 %all-to-all-done.4 = bf16[8,54,128]{2,1,0:T(8,128)(2,1)S(1)} async-done(((bf16[8,54,128]{2,1,0:T(8,128)(2,1)}), bf16[8,54,128]{2,1,0:T(8,128)(2,1)S(1)}, u32[]{:S(2)}, u32[]{:S(2)}) %all-to-all-start.4) | async-done | bytes 110624 | tf_op jit(solution)/shard_map/all_to_all | solution.py:334
  217.8 0.7 broadcast_in_dim.25
  218.5 3.4 %all-to-all-start.5 = ((bf16[8,54,128]{2,1,0:T(8,128)(2,1)}), bf16[8,54,128]{2,1,0:T(8,128)(2,1)S(1)}, u32[]{:S(2)}, u32[]{:S(2)}) async-start(bf16[8,54,128]{2,1,0:T(8,128)(2,1)} %broadcast_in_dim.25), calls=%async_computation.5 | async-start | bytes 229376 | tf_op jit(solution)/shard_map/all_to_all | solution.py:334
  221.9 7.6 %all-to-all-done.5 = bf16[8,54,128]{2,1,0:T(8,128)(2,1)S(1)} async-done(((bf16[8,54,128]{2,1,0:T(8,128)(2,1)}), bf16[8,54,128]{2,1,0:T(8,128)(2,1)S(1)}, u32[]{:S(2)}, u32[]{:S(2)}) %all-to-all-start.5) | async-done | bytes 110624 | tf_op jit(solution)/shard_map/all_to_all | solution.py:334
  230.2 8.0 %all-to-all-start.6 = ((bf16[8,54,128]{2,1,0:T(8,128)(2,1)}), bf16[8,54,128]{2,1,0:T(8,128)(2,1)S(1)}, u32[]{:S(2)}, u32[]{:S(2)}) async-start(bf16[8,54,128]{2,1,0:T(8,128)(2,1)} %broadcast_in_dim.26), calls=%async_computation.6 | async-start | bytes 229376 | tf_op jit(solution)/shard_map/all_to_all | solution.py:334
  238.2 1.4 all-gather.15.cloned.1.call-done.everyone
  239.6 2.5 %pick.1 = bf16[256,1152]{1,0:T(8,128)(2,1)} custom-call(s32[4]{0:T(128)S(1)} %multiply_add_fusion.starts, bf16[2048,1152]{1,0:T(8,128)(2,1)} %all-gather.15.cloned.1.call-done.everyone), custom_call_target="tpu_custom_call" | custom-call | flops 6000000000 | bytes 8000000 | tf_op jit(solution)/shard_map/pick/pallas_call | solution.py:446
  242.1 1.3 all-to-all-done.6
  (81 shorter events, 8.7 us)
Async XLA Ops:
  7.2 89.9 %all-gather.9.cloned.1.call-start = ((), (), s32[]{:S(2)}) async-start(), calls=%async_computation.7 | async-start | bytes 5640192 | tf_op jit(solution)/shard_map/all_gather | solution.py:386
  9.8 20.8 %copy-start.4 = (bf16[4,1,64,1152]{3,2,1,0:T(8,128)(2,1)S(1)}, bf16[4,1,64,1152]{3,2,1,0:T(8,128)(2,1)}, u32[]{:S(2)}) copy-start(bf16[4,1,64,1152]{3,2,1,0:T(8,128)(2,1)} %param.21) | copy-start | bytes 1769476
  13.1 37.0 %all-to-all-start = ((bf16[64,2,2688]{2,1,0:T(2,128)(2,1)}), bf16[64,2,2688]{2,1,0:T(2,128)(2,1)S(1)}, u32[]{:S(2)}, u32[]{:S(2)}) async-start(bf16[64,2,2688]{2,1,0:T(2,128)(2,1)} %broadcast_in_dim.19), calls=%async_computation | async-start | bytes 1376256 | tf_op jit(solution)/shard_map/all_to_all | solution.py:334
  30.2 71.0 %all-gather.11.cloned.1.call-start = ((), (), s32[]{:S(2)}) async-start(), calls=%async_computation.8 | async-start | bytes 5971968 | tf_op jit(solution)/shard_map/all_gather | solution.py:357
  53.5 92.1 %all-gather.13.cloned.1.call-start = ((), (), s32[]{:S(2)}) async-start(), calls=%async_computation.9 | async-start | bytes 5971968 | tf_op jit(solution)/shard_map/all_gather | solution.py:357
  95.7 1.1 copy-start.6
  95.7 5.5 %copy-start.1 = (f32[3,1152]{1,0:T(4,128)S(1)}, f32[3,1152]{1,0:T(4,128)}, u32[]{:S(2)}) copy-start(f32[3,1152]{1,0:T(4,128)} %gains.5) | copy-start | bytes 41476
  98.1 25.4 %copy-start.5 = (s32[4,4]{1,0:T(4,128)S(1)}, s32[4,4]{1,0:T(4,128)}, u32[]{:S(2)}) copy-start(s32[4,4]{1,0:T(4,128)} %param.14) | copy-start | bytes 196
  109.3 0.8 copy-start.2
  110.1 35.5 %copy-start = (f32[3,1152]{1,0:T(4,128)S(1)}, f32[3,1152]{1,0:T(4,128)}, u32[]{:S(2)}) copy-start(f32[3,1152]{1,0:T(4,128)} %gains.4) | copy-start | bytes 41476
  110.1 31.8 %all-to-all-start.2 = ((bf16[64,4,1152]{2,1,0:T(4,128)(2,1)}), bf16[64,4,1152]{2,1,0:T(4,128)(2,1)S(1)}, u32[]{:S(2)}, u32[]{:S(2)}) async-start(bf16[64,4,1152]{2,1,0:T(4,128)(2,1)} %get-tuple-element.18.mid), calls=%async_computation.2 | async-start | bytes 1179648 | tf_op jit(solution)/shard_map/all_to_all | solution.py:334
  123.3 116.3 %all-gather.15.cloned.1.call-start = ((), (), s32[]{:S(2)}) async-start(), calls=%async_computation.10 | async-start | bytes 5308416 | tf_op jit(solution)/shard_map/all_gather | solution.py:445
  157.6 38.0 %copy-start.3 = (bf16[256,1152]{1,0:T(8,128)(2,1)S(1)}, bf16[256,1152]{1,0:T(8,128)(2,1)}, u32[]{:S(2)}) copy-start(bf16[256,1152]{1,0:T(8,128)(2,1)} %copy-done.2) | copy-start | bytes 1769476
  195.6 8.3 %copy-start.7 = (s32[4]{0:T(128)S(1)}, s32[4]{0:T(128)}, u32[]{:S(2)}) copy-start(s32[4]{0:T(128)} %param.12) | copy-start | bytes 52
  204.9 12.9 %all-to-all-start.4 = ((bf16[8,54,128]{2,1,0:T(8,128)(2,1)}), bf16[8,54,128]{2,1,0:T(8,128)(2,1)S(1)}, u32[]{:S(2)}, u32[]{:S(2)}) async-start(bf16[8,54,128]{2,1,0:T(8,128)(2,1)} %broadcast_in_dim.24), calls=%async_computation.4 | async-start | bytes 229376 | tf_op jit(solution)/shard_map/all_to_all | solution.py:334
  218.5 11.0 %all-to-all-start.5 = ((bf16[8,54,128]{2,1,0:T(8,128)(2,1)}), bf16[8,54,128]{2,1,0:T(8,128)(2,1)S(1)}, u32[]{:S(2)}, u32[]{:S(2)}) async-start(bf16[8,54,128]{2,1,0:T(8,128)(2,1)} %broadcast_in_dim.25), calls=%async_computation.5 | async-start | bytes 229376 | tf_op jit(solution)/shard_map/all_to_all | solution.py:334
  230.2 13.2 %all-to-all-start.6 = ((bf16[8,54,128]{2,1,0:T(8,128)(2,1)}), bf16[8,54,128]{2,1,0:T(8,128)(2,1)S(1)}, u32[]{:S(2)}, u32[]{:S(2)}) async-start(bf16[8,54,128]{2,1,0:T(8,128)(2,1)} %broadcast_in_dim.26), calls=%async_computation.6 | async-start | bytes 229376 | tf_op jit(solution)/shard_map/all_to_all | solution.py:334
Sparse Core Ops, SparseCore 0:
  10.1 46.7 all-gather.8
  59.0 42.1 all-gather.10
  103.4 42.1 all-gather.12
  204.0 35.5 all-gather.14
